TPU v7x, 32 devices: a whole 2x2x4 slice. The times are simulated.
32 devices in a mesh: dp: 4 (over y, x), row: 4 (over z), col: 2 (over core).
Axes of the slice: x: 2, y: 2, z: 4, core: 2. Of those that a mesh axis runs over, the one named last changes fastest.
Arguments:
- queries: bfloat16 [4, 48, 32, 1024], P('dp', 'row', 'col'), may hold values from -6 to 6
- keyvals: bfloat16 [4, 2, 48, 32, 1024], P('dp', None, 'row', 'col'), may hold values from -6 to 6
- out_weight: bfloat16 [4, 1024, 2048], P('dp', ('row', 'col')), may hold values from -0.75 to 0.75
- gate_weight: bfloat16 [4, 2048, 2048], P('dp', ('row', 'col')), may hold values from -0.125 to 0.125
- class_table: bfloat16 [4, 1000, 2048], P('dp', None, ('row', 'col')), may hold values from -5 to 5
- labels: int32 [4], P('dp'), may hold values from 0 to 999
- timesteps: int32 [4], P('dp'), may hold values from 0 to 999
- round_index: int32 [1], replicated, may hold values from 0 to 996
Outputs:
- update: bfloat16 [4, 48, 32, 2048], P('dp', 'row', 'col')
All inputs are finite; a program needn't handle non-finite values.
Results may differ from a plain program's by a relative error of at most 0.0081.
Values may be sent and summed in bfloat16 or wider, within the bound.
A program may use at most 64 MiB of HBM per device.

v0:
```python
from functools import partial
import math

import jax
import jax.numpy as jnp
from jax import lax
from jax.sharding import PartitionSpec as P

HDIM = 128
RADIUS = 3


def shortened(value):

    def short(part):
        return part.astype(jnp.bfloat16) if part.dtype == jnp.float32 else part

    return jax.tree.map(short, value)


def from_behind(value, axis, steps):
    count = lax.axis_size(axis)
    pairs = [(source, (source + steps) % count) for source in range(count)]
    return lax.ppermute(value, axis, pairs)


def padded(value, sides, width):
    for axis, dim in sides:
        size, length = (lax.axis_size(axis), value.shape[dim])
        up = [(i, (i + 1) % size) for i in range(size - 1)]
        down = [(j, i) for i, j in up]
        last = lax.slice_in_dim(value, length - width, length, axis=dim)
        leading = lax.slice_in_dim(value, 0, width, axis=dim)
        before = lax.ppermute(last, axis, up)
        after = lax.ppermute(leading, axis, down)
        value = jnp.concatenate([before, value, after], axis=dim)
    return value


def gossip_from(packed, distance):
    return jax.tree.map(
        lambda part, own: part.astype(own.dtype),
        from_behind(shortened(packed), "dp", distance),
        packed,
    )


def local(queries, keyvals, out_weight, gate_weight, class_table, labels, timesteps, round_index):
    bit_count = lax.axis_size("dp").bit_length() - 1
    shard_inner = out_weight.shape[1]
    model_width = out_weight.shape[2]
    shard_width = gate_weight.shape[1]
    class_count = class_table.shape[1]
    packed = jnp.concatenate(
        [out_weight.reshape(-1), gate_weight.reshape(-1), class_table.reshape(-1)]
    )
    branches = [partial(gossip_from, distance=2**power) for power in range(bit_count)]
    peer_params = lax.switch(round_index[0] % bit_count, branches, packed)
    mixed = (0.5 * (packed.astype(jnp.float32) + peer_params.astype(jnp.float32))).astype(
        jnp.bfloat16
    )
    out_size = shard_inner * model_width
    gate_size = shard_width * model_width
    out_mixed = mixed[:out_size].reshape(shard_inner, model_width)
    gate_mixed = mixed[out_size : out_size + gate_size].reshape(shard_width, model_width)
    table_mixed = mixed[out_size + gate_size :].reshape(class_count, shard_width)
    half_width = model_width // 2
    positions = lax.axis_index(("row", "col")) * shard_width + jnp.arange(shard_width)
    freq_index = (positions % half_width).astype(jnp.float32)
    frequency = jnp.exp(-math.log(10000.0) * freq_index / half_width)
    angle_value = timesteps[0].astype(jnp.float32) * frequency
    embed = jnp.where(positions < half_width, jnp.cos(angle_value), jnp.sin(angle_value))
    class_row = lax.dynamic_index_in_dim(table_mixed, labels[0], 0, keepdims=False)
    cond = jax.nn.silu(class_row.astype(jnp.float32) + embed).astype(jnp.bfloat16)
    partial_gate = jnp.dot(cond[None, :], gate_mixed, preferred_element_type=jnp.float32)[0]
    gate = lax.psum(partial_gate, ("row", "col"))
    tile_rows = queries.shape[1]
    tile_cols = queries.shape[2]
    inner_width = queries.shape[3]
    head_count = inner_width // HDIM
    window = 2 * RADIUS + 1
    ext_cols = tile_cols + 2 * RADIUS
    local_kv = keyvals[0]
    extended = padded(local_kv, (("row", 1), ("col", 2)), RADIUS)
    banded = jnp.stack(
        [extended[:, offset : offset + tile_rows] for offset in range(window)], axis=2
    )
    banded = banded.reshape(2, tile_rows, window * ext_cols, head_count, HDIM)
    query_heads = queries[0].reshape(tile_rows, tile_cols, head_count, HDIM)
    score_scale = 1.0 / math.sqrt(HDIM)
    scores = (
        jnp.einsum("ijhd,ikhd->ihjk", query_heads, banded[0], preferred_element_type=jnp.float32)
        * score_scale
    )
    row_global = lax.axis_index("row") * tile_rows + jnp.arange(tile_rows + 2 * RADIUS) - RADIUS
    row_valid = (row_global >= 0) & (row_global < tile_rows * lax.axis_size("row"))
    row_band = jnp.stack(
        [row_valid[offset : offset + tile_rows] for offset in range(window)], axis=1
    )
    col_global = lax.axis_index("col") * tile_cols + jnp.arange(ext_cols) - RADIUS
    col_valid = (col_global >= 0) & (col_global < tile_cols * lax.axis_size("col"))
    reach = (
        jnp.abs(jnp.arange(ext_cols)[None, :] - jnp.arange(tile_cols)[:, None] - RADIUS) <= RADIUS
    )
    allowed = (
        row_band[:, None, None, :, None]
        & col_valid[None, None, None, None, :]
        & reach[None, None, :, None, :]
    )
    allowed = allowed.reshape(tile_rows, 1, tile_cols, window * ext_cols)
    scores = jnp.where(allowed, scores, jnp.float32(-1e30))
    row_max = jnp.max(scores, axis=-1, keepdims=True)
    exponent = jnp.exp(scores - row_max)
    probs = (exponent / jnp.sum(exponent, axis=-1, keepdims=True)).astype(jnp.bfloat16)
    attended = jnp.einsum("ihjk,ikhd->ijhd", probs, banded[1], preferred_element_type=jnp.float32)
    attended = attended.astype(jnp.bfloat16).reshape(tile_rows * tile_cols, inner_width)
    projected = jnp.dot(
        attended,
        lax.all_gather(out_mixed, ("row", "col"), axis=0, tiled=True),
        preferred_element_type=jnp.float32,
    )
    result = (gate[None, :] * projected).astype(jnp.bfloat16)
    return result.reshape(1, tile_rows, tile_cols, model_width)


def solution(mesh):
    placed = (
        P("dp", "row", "col", None),
        P("dp", None, "row", "col", None),
        P("dp", ("row", "col"), None),
        P("dp", ("row", "col"), None),
        P("dp", None, ("row", "col")),
        P("dp"),
        P("dp"),
        P(),
    )
    return jax.shard_map(
        local, mesh=mesh, in_specs=placed, out_specs=P("dp", "row", "col", None), check_vma=False
    )
```

profile of v0, /device:TPU:0, one launch (start us, length us, event | category | flops | bytes accessed | tf_op | source)
XLA Modules:
  0.0 146.9 jit_solution(2890975642599125272)
XLA Ops:
  6.5 0.0 copy-start.1
  6.5 0.0 all-gather.2.cloned.1.call-start
  7.3 1.1 copy.18
  8.4 0.8 constant_dynamic-update-slice_fusion
  9.3 1.4 copy.19
  10.7 0.0 copy-done.1
  10.7 0.4 copy.20
  11.1 1.0 constant_dynamic-update-slice_fusion.2
  12.2 0.8 constant_dynamic-update-slice_fusion.1
  13.0 48.6 %conditional.4 = (bf16[1042432]{0:T(1024)(128)(2,1)}) conditional(s32[]{:T(128)} %clamp.3, bf16[1042432]{0:T(1024)(128)(2,1)} %constant_dynamic-update-slice_fusion.1, bf16[1042432]{0:T(1024)(128)(2,1)} %constant_dynamic-update-slice_fusion.1), branch_computations={%region_0.1_spmd, %region_1.2_spmd} | conditional | bytes 8339504
  13.0 3.0 %collective-permute-start.1 = (bf16[1042432]{0:T(1024)(128)(2,1)}, bf16[1042432]{0:T(1024)(128)(2,1)}, u32[]{:S(2)}, u32[]{:S(2)}) collective-permute-start(bf16[1042432]{0:T(1024)(128)(2,1)} %param.1), channel_id=1, source_target_pairs={{0,16},{8,24},{16,0},{24,8},{1,17},{9,25},{17,1},{25,9},{2,18},{10... | collective-permute-start | bytes 6254600 | tf_op jit(solution)/shard_map/cond/branch_1_fun/ppermute | solution.py:24
  16.0 45.7 %collective-permute-done.1 = bf16[1042432]{0:T(1024)(128)(2,1)} collective-permute-done((bf16[1042432]{0:T(1024)(128)(2,1)}, bf16[1042432]{0:T(1024)(128)(2,1)}, u32[]{:S(2)}, u32[]{:S(2)}) %collective-permute-start.1) | collective-permute-done | bytes 2084896 | tf_op jit(solution)/shard_map/cond/branch_1_fun/ppermute | solution.py:24
  61.7 0.0 copy-start
  61.7 2.9 %multiply_convert_fusion = bf16[1042432]{0:T(1024)(128)(2,1)S(1)} fusion(bf16[1042432]{0:T(1024)(128)(2,1)} %get-tuple-element.31, bf16[1042432]{0:T(1024)(128)(2,1)} %constant_dynamic-update-slice_fusion.1), kind=kLoop, calls=%fused_computation.1 | loop fusion | flops 5212160 | bytes 6254592 | tf_op jit(solution)/shard_map/convert_element_type | solution.py:59
  64.6 1.0 slice.126
  65.6 0.0 all-gather.2.cloned.1.call-update
  65.6 0.0 copy-done
  65.7 0.8 fusion.59
  66.4 4.4 %collective-permute-start.2 = (bf16[2,3,16,1024]{3,2,1,0:T(8,128)(2,1)}, bf16[2,3,16,1024]{3,2,1,0:T(8,128)(2,1)}, u32[]{:S(2)}, u32[]{:S(2)}) collective-permute-start(bf16[2,3,16,1024]{3,2,1,0:T(8,128)(2,1)} %get-tuple-element.20), channel_id=1, source_target_pairs={{0,2},{2,4},{4,6},{1,3},{3,5},{5,7},{8,10},{10,12},{12,14},{9,11},... | collective-permute-start | bytes 589832 | tf_op jit(solution)/shard_map/ppermute | solution.py:34
  70.8 1.3 collective-permute-start.3
  72.1 1.0 slice.128
  73.2 0.1 slice_bitcast_fusion.7
  73.3 0.1 copy.12
  73.4 0.1 and.85
  73.5 0.1 and.86
  73.7 0.1 and.89
  73.8 0.1 and.94
  73.9 1.1 copy.21
  75.0 1.7 %slice.104 = bf16[256,2048]{1,0:T(8,128)(2,1)S(1)} reshape(bf16[524288]{0:T(1024)(128)(2,1)} %slice.128) | data formatting | bytes 2097152 | tf_op jit(solution)/shard_map/slice | solution.py:65
  76.6 0.2 slice.102
  78.1 0.3 fusion.33
  78.4 17.3 %psum.7 = f32[2048]{0:T(1024)S(1)} all-reduce(f32[2048]{0:T(1024)S(1)} %bitcast.93), channel_id=1, replica_groups=mesh['dp'=4,'row'=4,'col'=2] {'row','col'}, use_global_device_ids=true, to_apply=%region_2.3 | all-reduce | flops 2048 | bytes 16384 | tf_op jit(solution)/shard_map/psum | solution.py:76
  95.8 0.0 collective-permute-done.2
  95.8 0.0 collective-permute-done.3
  95.8 1.3 pad_maximum_fusion.3
  97.1 1.3 collective-permute-start.4
  98.4 1.3 collective-permute-start.5
  99.7 0.0 collective-permute-done.4
  99.7 2.1 %collective-permute-done.5 = bf16[2,18,3,1024]{3,2,1,0:T(4,128)(2,1)S(1)} collective-permute-done((bf16[2,18,3,1024]{3,2,1,0:T(4,128)(2,1)S(1)}, bf16[2,18,3,1024]{3,2,1,0:T(4,128)(2,1)S(1)}, u32[]{:S(2)}, u32[]{:S(2)}) %collective-permute-start.5) | collective-permute-done | bytes 221216 | tf_op jit(solution)/shard_map/ppermute | solution.py:35
  101.9 1.9 %pad_maximum_fusion = bf16[2,18,22,1024]{3,2,1,0:T(8,128)(2,1)S(1)} fusion(bf16[2,18,3,1024]{3,2,1,0:T(4,128)(2,1)S(1)} %collective-permute-done.5, bf16[2,3,16,1024]{3,2,1,0:T(8,128)(2,1)} %collective-permute-done.3, bf16[2,12,16,1024]{3,2,1,0:T(8,128)(2,1)S(1)} %bitcast.83, bf16[2,3,16,1024]{3,2,1,0:T(8,128)(2,1)} %collective-permute-done.2, ...), kind=kLoop, calls=%fused_computation.8 | loop fusion | flops 8110080 | bytes 3244032 | tf_op jit(solution)/shard_map/concatenate | solution.py:36
  103.8 0.1 fusion.22
  103.9 0.1 fusion.21
  104.0 0.1 fusion.20
  104.1 0.1 fusion.19
  104.2 0.1 fusion.18
  104.3 0.1 fusion.17
  104.4 0.1 fusion.16
  104.4 2.5 %fusion.58 = (bf16[1,12,7,22,1024]{4,3,1,0,2:T(8,128)(2,1)S(1)}, bf16[1,12,7,22,1024]{4,3,1,0,2:T(8,128)(2,1)}) fusion(bf16[2,12,7,22,1024]{4,3,1,0,2:T(8,128)(2,1)S(1)} %fusion.16), kind=kLoop, calls=%fused_computation.85 | loop fusion | bytes 15138816 | tf_op jit(solution)/shard_map/slice | solution.py:92
  106.9 2.4 %copy.13 = bf16[1,12,7,22,1024]{4,3,2,1,0:T(8,128)(2,1)} copy(bf16[1,12,7,22,1024]{4,3,1,0,2:T(8,128)(2,1)S(1)} %get-tuple-element.16) | data formatting | bytes 7569408 | tf_op jit(solution)/shard_map/slice | solution.py:92
  109.3 7.2 %squeeze.23 = bf16[12,154,8,128]{3,2,1,0:T(8,128)(2,1)} reshape(bf16[1,12,7,22,1024]{4,3,2,1,0:T(8,128)(2,1)} %copy.13) | data formatting | bytes 7569408 | tf_op jit(solution)/shard_map/squeeze | solution.py:92
  116.5 4.6 %copy.11 = bf16[1,12,7,22,1024]{4,3,2,1,0:T(8,128)(2,1)} copy(bf16[1,12,7,22,1024]{4,3,1,0,2:T(8,128)(2,1)} %get-tuple-element.17) | data formatting | bytes 7569408 | tf_op jit(solution)/shard_map/slice | solution.py:115
  121.0 7.2 %squeeze.22 = bf16[12,154,8,128]{3,2,1,0:T(8,128)(2,1)} reshape(bf16[1,12,7,22,1024]{4,3,2,1,0:T(8,128)(2,1)} %copy.11) | data formatting | bytes 7569408 | tf_op jit(solution)/shard_map/squeeze | solution.py:115
  128.2 4.4 %fusion.60 = (f32[12,8,16]{2,1,0:T(8,128)S(1)}, f32[12,8,16,154]{3,2,1,0:T(8,128)S(1)}) fusion(bf16[12,154,8,128]{3,2,1,0:T(8,128)(2,1)} %squeeze.23, pred[12,16,154]{2,1,0:T(8,128)(4,1)S(1)} %broadcast_and_fusion, bf16[12,16,8,128]{3,2,1,0:T(8,128)(2,1)S(1)} %bitcast.91), kind=kOutput, calls=%fused_computation.87 | convolution fusion | flops 61501592 | bytes 5159808 | tf_op jit(solution)/shard_map/sub | solution.py:113
  132.6 3.3 %fusion.13 = bf16[12,16,8,128]{3,1,2,0:T(8,128)(2,1)S(1)} fusion(bf16[12,154,8,128]{3,2,1,0:T(8,128)(2,1)} %squeeze.22, f32[12,8,16,154]{3,2,1,0:T(8,128)S(1)} %get-tuple-element.30, f32[12,8,16]{2,1,0:T(8,128)S(1)} %get-tuple-element.29), kind=kOutput, calls=%fused_computation.14 | convolution fusion | flops 61224960 | bytes 5130240 | tf_op jit(solution)/shard_map/ihjk,ikhd->ijhd/dot_general | solution.py:115
  135.9 0.1 copy.17
  136.0 0.0 all-gather.2.cloned.1.call-done
  136.0 4.1 %fusion.5 = bf16[192,2048]{1,0:T(8,128)(2,1)} fusion(bf16[1024,2048]{1,0:T(8,128)(2,1)} %all-gather.2.cloned.1.call-done, f32[2048]{0:T(1024)S(1)} %psum.7, bf16[24,8,8,128]{3,2,1,0:T(8,128)(2,1)S(1)} %bitcast.92), kind=kOutput, calls=%fused_computation.7 | convolution fusion | flops 806092800 | bytes 5382144 | tf_op jit(solution)/shard_map/dot_general | solution.py:117
  (10 shorter events, 0.2 us)
Async XLA Ops:
  6.5 4.2 %copy-start.1 = (bf16[1,1000,256]{2,1,0:T(8,128)(2,1)S(1)}, bf16[1,1000,256]{2,1,0:T(8,128)(2,1)}, u32[]{:S(2)}) copy-start(bf16[1,1000,256]{2,1,0:T(8,128)(2,1)} %param.14) | copy-start | bytes 1536004
  6.5 129.5 %all-gather.2.cloned.1.call-start = ((), (), s32[]{:S(2)}) async-start(), calls=%async_computation | async-start | bytes 4718592 | tf_op jit(solution)/shard_map/all_gather | solution.py:119
  13.0 48.6 %collective-permute-start.1 = (bf16[1042432]{0:T(1024)(128)(2,1)}, bf16[1042432]{0:T(1024)(128)(2,1)}, u32[]{:S(2)}, u32[]{:S(2)}) collective-permute-start(bf16[1042432]{0:T(1024)(128)(2,1)} %param.1), channel_id=1, source_target_pairs={{0,16},{8,24},{16,0},{24,8},{1,17},{9,25},{17,1},{25,9},{2,18},{10... | collective-permute-start | bytes 6254600 | tf_op jit(solution)/shard_map/cond/branch_1_fun/ppermute | solution.py:24
  61.7 4.0 %copy-start = (bf16[1,2,12,16,1024]{4,3,2,1,0:T(8,128)(2,1)S(1)}, bf16[1,2,12,16,1024]{4,3,2,1,0:T(8,128)(2,1)}, u32[]{:S(2)}) copy-start(bf16[1,2,12,16,1024]{4,3,2,1,0:T(8,128)(2,1)} %param.11) | copy-start | bytes 2359300
  66.4 29.3 %collective-permute-start.2 = (bf16[2,3,16,1024]{3,2,1,0:T(8,128)(2,1)}, bf16[2,3,16,1024]{3,2,1,0:T(8,128)(2,1)}, u32[]{:S(2)}, u32[]{:S(2)}) collective-permute-start(bf16[2,3,16,1024]{3,2,1,0:T(8,128)(2,1)} %get-tuple-element.20), channel_id=1, source_target_pairs={{0,2},{2,4},{4,6},{1,3},{3,5},{5,7},{8,10},{10,12},{12,14},{9,11},... | collective-permute-start | bytes 589832 | tf_op jit(solution)/shard_map/ppermute | solution.py:34
  70.8 24.9 %collective-permute-start.3 = (bf16[2,3,16,1024]{3,2,1,0:T(8,128)(2,1)}, bf16[2,3,16,1024]{3,2,1,0:T(8,128)(2,1)}, u32[]{:S(2)}, u32[]{:S(2)}) collective-permute-start(bf16[2,3,16,1024]{3,2,1,0:T(8,128)(2,1)} %get-tuple-element.21), channel_id=1, source_target_pairs={{2,0},{4,2},{6,4},{3,1},{5,3},{7,5},{10,8},{12,10},{14,12},{11,9},... | collective-permute-start | bytes 589832 | tf_op jit(solution)/shard_map/ppermute | solution.py:35
  97.1 2.7 %collective-permute-start.4 = (bf16[2,18,3,1024]{3,2,1,0:T(4,128)(2,1)S(1)}, bf16[2,18,3,1024]{3,2,1,0:T(4,128)(2,1)S(1)}, u32[]{:S(2)}, u32[]{:S(2)}) collective-permute-start(bf16[2,18,3,1024]{3,2,1,0:T(4,128)(2,1)S(1)} %get-tuple-element.18), channel_id=1, source_target_pairs={{0,1},{2,3},{4,5},{6,7},{8,9},{10,11},{12,13},{14,15},{16,17},{18,... | collective-permute-start | bytes 663560 | tf_op jit(solution)/shard_map/ppermute | solution.py:34
  98.4 3.5 %collective-permute-start.5 = (bf16[2,18,3,1024]{3,2,1,0:T(4,128)(2,1)S(1)}, bf16[2,18,3,1024]{3,2,1,0:T(4,128)(2,1)S(1)}, u32[]{:S(2)}, u32[]{:S(2)}) collective-permute-start(bf16[2,18,3,1024]{3,2,1,0:T(4,128)(2,1)S(1)} %get-tuple-element.19), channel_id=1, source_target_pairs={{1,0},{3,2},{5,4},{7,6},{9,8},{11,10},{13,12},{15,14},{17,16},{19,... | collective-permute-start | bytes 663560 | tf_op jit(solution)/shard_map/ppermute | solution.py:35
Sparse Core Ops, SparseCore 0:
  65.8 49.3 all-gather.1
where the time goes:
time: 148 us; the launch traced here: 147 us
  waiting for transfers between devices  47.9 us (32%)
  local copies, waits for them, and re-layouts  36.6 us (25%)
  blocking collectives  17.3 us (12%)
  between operations  15.7 us (11%)
  matrix products  12 us (8%)
  starting transfers between devices  11.2 us (8%)
  other arithmetic  6.2 us (4%)
    ppermute x1, waiting for transfers between devices, from_behind(): return lax.ppermute(value, axis, pairs)  45.7 us
    psum x1, blocking collectives, local(): gate = lax.psum(partial_gate, ('row', 'col'))  17.3 us
    squeeze x1, local copies, waits for them, and re-layouts, local(): banded[0]  7.17 us
    squeeze x1, local copies, waits for them, and re-layouts, local(): banded[1]  7.16 us
    unnamed x16, local copies, waits for them, and re-layouts  6.48 us
    ppermute x2, starting transfers between devices, padded(): before = lax.ppermute(last, axis, up)  5.68 us
    slice x2, local copies, waits for them, and re-layouts, local(): banded[0]  4.86 us
    slice x1, local copies, waits for them, and re-layouts, local(): banded[1]  4.57 us
  transfers between devices with their start and end apart: 6, of which 2 were waited for; matrix products, arithmetic and copies ran while one was open for 28% of the time, Pallas kernels for 0%

commit v1 on v0

v1 whole, which is shorter than its diff:
```python
import functools
import math

import jax
import jax.numpy as jnp
from jax import lax
from jax.experimental import pallas as pl
from jax.experimental.pallas import tpu as pltpu
from jax.sharding import PartitionSpec as P

HDIM = 128
RADIUS = 3
CHUNKS = 4
GROUP = 4
MESH = pl.DeviceIdType.MESH
F32 = jnp.float32
BF16 = jnp.bfloat16


def remote(src, dst, send, recv, **where):
    return pltpu.make_async_remote_copy(
        src_ref=src, dst_ref=dst, send_sem=send, recv_sem=recv, device_id=where, device_id_type=MESH
    )


def kernel(
    sizes, distance,
    q_hbm, kv_hbm, o_hbm, g_hbm, t_hbm, label_ref, step_ref,
    out_hbm,
    q_buf, kv_buf, bias, att, o_own, o_peer, w_buf, out_buf, g_buf, t_buf,
    pack_out, pack_in, reply_out, reply_in, gates,
    local_sem, out_sem, gossip_send, gossip_recv, w_up, w_down, w_side, w_recv,
    halo_send, halo_recv, side_send, side_recv, note_send, note_recv, gate_send, gate_recv,
):
    n_dp, n_row, n_col = sizes
    group = n_row * n_col
    tile_rows, tile_cols, inner = kv_hbm.shape[2:]
    shard, width = o_hbm.shape[1:]
    cut = width // CHUNKS
    span = t_hbm.shape[2]
    slot = pack_out.shape[1] // 3
    classes = t_hbm.shape[1]
    heads = inner // HDIM
    sides = [1] if n_col == 2 else [n_col - 1, 1]
    wide = kv_buf.shape[2]

    p, r, c = lax.axis_index("dp"), lax.axis_index("row"), lax.axis_index("col")
    me = r * n_col + c
    ahead, behind = lax.rem(p + distance, n_dp), lax.rem(p + n_dp - distance, n_dp)
    has_up, has_down = r > 0, r < n_row - 1

    def col_of(step):
        return lax.rem(c + step, n_col)

    loads = [
        pltpu.make_async_copy(t_hbm.at[0], t_buf, local_sem.at[0]),
        pltpu.make_async_copy(o_hbm.at[0], o_own, local_sem.at[1]),
        pltpu.make_async_copy(g_hbm.at[0], g_buf, local_sem.at[2]),
        pltpu.make_async_copy(q_hbm.at[0], q_buf, local_sem.at[3]),
        pltpu.make_async_copy(
            kv_hbm.at[0], kv_buf.at[:, pl.ds(RADIUS, tile_rows), pl.ds(0, tile_cols)], local_sem.at[4]
        ),
    ]
    for load in loads:
        load.start()

    barrier = pltpu.get_barrier_semaphore()
    for step in range(1, group):
        other = lax.rem(me + step, group)
        pl.semaphore_signal(
            barrier, inc=1, device_id={"row": other // n_col, "col": lax.rem(other, n_col)}, device_id_type=MESH
        )
    pl.semaphore_signal(barrier, inc=1, device_id={"dp": ahead}, device_id_type=MESH)
    greeted = group
    if (2 * distance) % n_dp:
        pl.semaphore_signal(barrier, inc=1, device_id={"dp": behind}, device_id_type=MESH)
        greeted += 1
    pl.semaphore_wait(barrier, greeted)

    def halo(which):
        first, place = ((0, tile_rows + RADIUS), (tile_rows - RADIUS, 0))[which]
        return remote(
            kv_hbm.at[0, :, pl.ds(first, RADIUS)],
            kv_buf.at[:, pl.ds(place, RADIUS), pl.ds(0, tile_cols)],
            halo_send.at[which], halo_recv.at[which], row=(r - 1, r + 1)[which],
        )

    def side(i):
        return remote(
            kv_hbm.at[0],
            kv_buf.at[:, pl.ds(RADIUS, tile_rows), pl.ds((i + 1) * tile_cols, tile_cols)],
            side_send.at[0, i], side_recv.at[0, i], col=col_of(sides[i]),
        )

    def corner(which, i):
        place = (tile_rows + RADIUS, 0)[which]
        rows = pl.ds(place, RADIUS)
        return remote(
            kv_buf.at[:, rows, pl.ds(0, tile_cols)],
            kv_buf.at[:, rows, pl.ds((i + 1) * tile_cols, tile_cols)],
            side_send.at[1 + which, i], side_recv.at[1 + which, i], col=col_of(sides[i]),
        )

    def gossip(k):
        return remote(
            o_hbm.at[0, :, pl.ds(k * cut, cut)], o_peer.at[k], gossip_send.at[k], gossip_recv.at[k], dp=ahead
        )

    gossip(0).start()
    pl.when(has_up)(lambda: halo(0).start())
    pl.when(has_down)(lambda: halo(1).start())
    for k in range(1, CHUNKS):
        gossip(k).start()
    for i in range(len(sides)):
        side(i).start()

    def class_row(label):
        rows = lax.broadcasted_iota(jnp.int32, (classes, span), 0).astype(F32)
        table = t_buf[...].astype(F32)
        return jnp.sum(jnp.where(rows == label, table, 0.0), axis=0, keepdims=True)

    loads[0].wait()
    label_here = jnp.full((1, span), label_ref[0], jnp.int32).astype(F32)
    pack_out[:, pl.ds(0, span)] = label_here
    pack_out[:, pl.ds(slot, span)] = jnp.full((1, span), step_ref[0], jnp.int32).astype(F32)
    pack_out[:, pl.ds(2 * slot, span)] = class_row(label_here)
    ask = remote(pack_out, pack_in, note_send.at[0], note_recv.at[0], dp=behind)
    ask.start()

    def w_copy(owner, k, sem, **where):
        rows = pl.ds(pl.multiple_of(owner * shard, shard), shard)
        place = w_buf.at[k, rows]
        return remote(place, place, sem, w_recv.at[owner, k], **where)

    def up_copy(row, k):
        return w_copy(row * n_col + c, k, w_up.at[row, k], row=r - 1)

    def down_copy(row, k):
        return w_copy(row * n_col + c, k, w_down.at[row, k], row=r + 1)

    def side_copy(row, k, step):
        return w_copy(row * n_col + c, k, w_side.at[step - 1, row, k], col=col_of(step))

    def spread(row, k):
        for step in range(1, n_col):
            side_copy(row, k, step).start()

    def own_chunk(k):
        gossip(k).wait_recv()
        both = o_own[:, pl.ds(k * cut, cut)].astype(F32) + o_peer[k].astype(F32)
        w_buf[k, pl.ds(pl.multiple_of(me * shard, shard), shard), :] = (0.5 * both).astype(BF16)
        pl.when(has_up)(lambda: up_copy(r, k).start())
        pl.when(has_down)(lambda: down_copy(r, k).start())
        spread(r, k)

    loads[1].wait()
    own_chunk(0)

    def against_gate(cond):
        tall = jnp.broadcast_to(cond, (16, span)).astype(BF16)
        return jnp.dot(tall, g_buf[...], preferred_element_type=F32)[0:1]

    half = width // 2
    position = me * span + lax.broadcasted_iota(jnp.int32, (1, span), 1)
    freq_index = jnp.where(position < half, position, position - half).astype(F32)
    frequency = jnp.exp(-math.log(10000.0) * freq_index / half)
    ask.wait_recv()
    mixed_row = 0.5 * (pack_in[:, pl.ds(2 * slot, span)] + class_row(pack_in[:, pl.ds(0, span)]))
    angle = pack_in[:, pl.ds(slot, span)] * frequency
    embed = jnp.where(position < half, jnp.cos(angle), jnp.sin(angle))
    value = mixed_row.astype(BF16).astype(F32) + embed
    cond = (value / (1.0 + jnp.exp(-value))).astype(BF16).astype(F32)
    loads[2].wait()
    reply_out[:, pl.ds(0, width)] = against_gate(cond)
    reply_out[:, pl.ds(width, span)] = cond
    answer = remote(reply_out, reply_in, note_send.at[1], note_recv.at[1], dp=ahead)
    answer.start()

    own_chunk(1)

    edge = jnp.zeros((2, RADIUS, wide, inner), BF16)

    @pl.when(jnp.logical_not(has_up))
    def _():
        kv_buf[:, pl.ds(0, RADIUS)] = edge

    @pl.when(jnp.logical_not(has_down))
    def _():
        kv_buf[:, pl.ds(tile_rows + RADIUS, RADIUS)] = edge

    n_q, n_k = GROUP * tile_cols, (GROUP + 2 * RADIUS) * wide
    blocks = wide // tile_cols
    q_index = lax.broadcasted_iota(jnp.int32, (n_q, n_k), 0)
    k_index = lax.broadcasted_iota(jnp.int32, (n_q, n_k), 1)
    q_row, q_col = q_index // tile_cols, lax.rem(q_index, tile_cols)
    k_block = k_index // tile_cols
    k_row = (k_block * -(-512 // blocks)) // 512
    k_block = k_block - k_row * blocks
    k_col = lax.rem(k_index, tile_cols)
    if n_col == 2:
        k_shift = jnp.where(k_block == 1, 1 - 2 * c, 0)
    else:
        k_shift = jnp.where(k_block == 1, 1, jnp.where(k_block == 2, -1, 0))
    k_col = k_col + k_shift * tile_cols
    near = (jnp.abs(k_col - q_col) <= RADIUS) & (k_row >= q_row) & (k_row <= q_row + 2 * RADIUS)
    k_col = k_col + c * tile_cols
    near = near & (k_col >= 0) & (k_col < n_col * tile_cols)
    for g in range(tile_rows // GROUP):
        row_here = k_row + (r * tile_rows + g * GROUP - RADIUS)
        seen = near & (row_here >= 0) & (row_here < n_row * tile_rows)
        bias[g] = seen.astype(F32)

    @pl.when(has_down)
    def _():
        halo(0).wait_recv()
        for i in range(len(sides)):
            corner(0, i).start()

    @pl.when(has_up)
    def _():
        halo(1).wait_recv()
        for i in range(len(sides)):
            corner(1, i).start()

    own_chunk(2)

    answer.wait_recv()
    share = 0.5 * (reply_in[:, pl.ds(0, width)] + against_gate(reply_in[:, pl.ds(width, span)]))
    gates[me] = share

    def gate_copy(owner, step):
        other = lax.rem(me + step, group)
        return remote(
            gates.at[owner], gates.at[owner], gate_send.at[step - 1], gate_recv.at[owner],
            row=other // n_col, col=lax.rem(other, n_col),
        )

    for step in range(1, group):
        gate_copy(me, step).start()

    for k in range(3, CHUNKS):
        own_chunk(k)

    loads[3].wait()
    loads[4].wait()
    for i in range(len(sides)):
        side(i).wait_recv()
        pl.when(has_down)(lambda i=i: corner(0, i).wait_recv())
        pl.when(has_up)(lambda i=i: corner(1, i).wait_recv())

    scale = 1.0 / math.sqrt(HDIM)

    def attend(head):
        lanes = pl.ds(pl.multiple_of(head * HDIM, HDIM), HDIM)
        for g in range(tile_rows // GROUP):
            rows = pl.ds(g * GROUP, GROUP)
            near_rows = pl.ds(g * GROUP, GROUP + 2 * RADIUS)
            query = q_buf[rows, :, lanes].reshape(n_q, HDIM)
            key = kv_buf[0, near_rows, :, lanes].reshape(n_k, HDIM)
            val = kv_buf[1, near_rows, :, lanes].reshape(n_k, HDIM)
            score = lax.dot_general(query, key, (((1,), (1,)), ((), ())), preferred_element_type=F32)
            score = jnp.where(bias[g] > 0.5, score, -1e30)
            top = jnp.max(score, axis=1, keepdims=True)
            weight = jnp.exp((score - top) * scale)
            total = jnp.sum(weight, axis=1, keepdims=True)
            mean = jnp.dot(weight.astype(BF16), val, preferred_element_type=F32) / total
            att[pl.ds(g * n_q, n_q), lanes] = mean.astype(BF16)

    def event(e, carry):
        hop, k = e // CHUNKS + 1, lax.rem(e, CHUNKS)

        @pl.when(r + hop < n_row)
        def _():
            row = r + hop
            up_copy(row, k).wait_recv()
            pl.when(has_up)(lambda: up_copy(row, k).start())
            spread(row, k)

        @pl.when((r - hop >= 0) & (hop < n_row))
        def _():
            row = r - hop
            down_copy(row, k).wait_recv()
            pl.when(has_down)(lambda: down_copy(row, k).start())
            spread(row, k)

        pl.when(e < heads)(lambda: attend(e))
        return carry

    before_last = max(heads, (n_row - 2) * CHUNKS)
    lax.fori_loop(0, before_last, event, 0)

    for step in range(1, group):
        owner = lax.rem(me + step, group)
        gate_copy(owner, step).wait_recv()
    gate = gates[0]
    for i in range(1, group):
        gate = gate + gates[i]

    def out_copy(k):
        return pltpu.make_async_copy(out_buf.at[k], out_hbm.at[:, pl.ds(k * cut, cut)], out_sem.at[k])

    for k in range(CHUNKS):
        e = (n_row - 2) * CHUNKS + k
        if e >= before_last:
            event(e, 0)
        for row in range(n_row):
            for step in range(1, n_col):
                owner = row * n_col + col_of(step)
                w_copy(owner, k, w_side.at[step - 1, row, k], col=col_of(step)).wait_recv()
        product = jnp.dot(att[...], w_buf[k], preferred_element_type=F32)
        out_buf[k] = (gate[:, k * cut : (k + 1) * cut] * product).astype(BF16)
        out_copy(k).start()

    for k in range(CHUNKS):
        out_copy(k).wait()
        gossip(k).wait_send()
        for row in range(n_row):
            pl.when(has_up & (r <= row))(lambda row=row, k=k: up_copy(row, k).wait_send())
            pl.when(has_down & (r >= row))(lambda row=row, k=k: down_copy(row, k).wait_send())
            for step in range(1, n_col):
                side_copy(row, k, step).wait_send()
    pl.when(has_up)(lambda: halo(0).wait_send())
    pl.when(has_down)(lambda: halo(1).wait_send())
    for i in range(len(sides)):
        side(i).wait_send()
        pl.when(has_down)(lambda i=i: corner(0, i).wait_send())
        pl.when(has_up)(lambda i=i: corner(1, i).wait_send())
    ask.wait_send()
    answer.wait_send()
    for step in range(1, group):
        gate_copy(me, step).wait_send()


def layer(sizes, distance, number, queries, keyvals, out_weight, gate_weight, class_table, labels, timesteps):
    n_dp, n_row, n_col = sizes
    group = n_row * n_col
    _, tile_rows, tile_cols, inner = queries.shape
    _, shard, width = out_weight.shape
    span = gate_weight.shape[1]
    classes = class_table.shape[1]
    cut = width // CHUNKS
    slot = max(span, 128)
    n_side = 1 if n_col == 2 else 2
    wide = tile_cols * (1 + n_side)
    tokens = tile_rows * tile_cols
    n_q, n_k = GROUP * tile_cols, (GROUP + 2 * RADIUS) * wide
    dma = pltpu.SemaphoreType.DMA
    return pl.pallas_call(
        functools.partial(kernel, sizes, distance),
        out_shape=jax.ShapeDtypeStruct((tokens, width), BF16),
        in_specs=[pl.BlockSpec(memory_space=pl.ANY)] * 5 + [pl.BlockSpec(memory_space=pltpu.SMEM)] * 2,
        out_specs=pl.BlockSpec(memory_space=pl.ANY),
        scratch_shapes=[
            pltpu.VMEM((tile_rows, tile_cols, inner), BF16),
            pltpu.VMEM((2, tile_rows + 2 * RADIUS, wide, inner), BF16),
            pltpu.VMEM((tile_rows // GROUP, n_q, n_k), F32),
            pltpu.VMEM((tokens, inner), BF16),
            pltpu.VMEM((shard, width), BF16),
            pltpu.VMEM((CHUNKS, shard, cut), BF16),
            pltpu.VMEM((CHUNKS, group * shard, cut), BF16),
            pltpu.VMEM((CHUNKS, tokens, cut), BF16),
            pltpu.VMEM((span, width), BF16),
            pltpu.VMEM((classes, span), BF16),
            pltpu.VMEM((1, 3 * slot), F32),
            pltpu.VMEM((1, 3 * slot), F32),
            pltpu.VMEM((1, width + slot), F32),
            pltpu.VMEM((1, width + slot), F32),
            pltpu.VMEM((group, 1, width), F32),
            dma((5,)),
            dma((CHUNKS,)),
            dma((CHUNKS,)),
            dma((CHUNKS,)),
            dma((n_row, CHUNKS)),
            dma((n_row, CHUNKS)),
            dma((n_col - 1, n_row, CHUNKS)),
            dma((group, CHUNKS)),
            dma((2,)),
            dma((2,)),
            dma((3, n_side)),
            dma((3, n_side)),
            dma((2,)),
            dma((2,)),
            dma((group - 1,)),
            dma((group,)),
        ],
        compiler_params=pltpu.CompilerParams(
            collective_id=number, has_side_effects=True, vmem_limit_bytes=48 * 2**20
        ),
        cost_estimate=pl.CostEstimate(flops=2 * tokens * inner * width, bytes_accessed=2**22, transcendentals=0),
        name=f"sublayer_distance_{distance}",
    )(queries, keyvals, out_weight, gate_weight, class_table, labels, timesteps)


def solution(mesh):
    sizes = tuple(mesh.shape[name] for name in ("dp", "row", "col"))
    bit_count = sizes[0].bit_length() - 1

    def local(queries, keyvals, out_weight, gate_weight, class_table, labels, timesteps, round_index):
        branches = [functools.partial(layer, sizes, 2**power, power) for power in range(bit_count)]
        operands = (queries, keyvals, out_weight, gate_weight, class_table, labels, timesteps)
        result = lax.switch(round_index[0] % bit_count, branches, *operands)
        return result.reshape(queries.shape[:3] + (out_weight.shape[2],))

    placed = (
        P("dp", "row", "col", None),
        P("dp", None, "row", "col", None),
        P("dp", ("row", "col"), None),
        P("dp", ("row", "col"), None),
        P("dp", None, ("row", "col")),
        P("dp"),
        P("dp"),
        P(),
    )
    return jax.shard_map(
        local, mesh=mesh, in_specs=placed, out_specs=P("dp", "row", "col", None), check_vma=False
    )
```

time: 148 us -> 58.2 us (0.39)
  Pallas kernels: 0 us -> 56.4 us
  waiting for transfers between devices: 47.9 us -> 0 us
  local copies, waits for them, and re-layouts: 36.6 us -> 0.88 us
  blocking collectives: 17.3 us -> 0 us
  between operations: 15.7 us -> 0.68 us
  matrix products: 12 us -> 0 us
  starting transfers between devices: 11.2 us -> 0 us
  other arithmetic: 6.2 us -> 0 us
    pallas_call x0 -> x1, Pallas kernels: none -> 56.4 us  [layer(): pl.pallas_call(functools.partial(kernel, sizes, distance), out_shape=jax....]
    ppermute x5 -> x0, waiting for transfers between devices: 47.8 us -> none  [the longest x1 45.7 us: from_behind(): return lax.ppermute(value, axis, pairs)]
    psum x1 -> x0, blocking collectives: 17.3 us -> none  [local(): gate = lax.psum(partial_gate, ('row', 'col'))]
    squeeze x2 -> x0, local copies, waits for them, and re-layouts: 14.3 us -> none  [the longest x1 7.17 us: local(): banded[0]]
    slice x10 -> x0, local copies, waits for them, and re-layouts: 14.2 us -> none  [the longest x2 4.86 us: local(): banded[0]]
    ppermute x5 -> x0, starting transfers between devices: 11.2 us -> none  [the longest x2 5.68 us: padded(): before = lax.ppermute(last, axis, up)]
    dot_general x3 -> x0, matrix products: 7.62 us -> none  [the longest x1 4.06 us: local(): jnp.dot(attended, lax.all_gather(out_mixed, ('row', 'col'), axis=0, tiled...]
    unnamed x16 -> x1, local copies, waits for them, and re-layouts: 6.48 us -> 0.88 us
  transfers between devices with their start and end apart: 6 -> 0, of which waited for: 2 -> 0; matrix products, arithmetic and copies ran while one was open for 28% -> 0% of each run, Pallas kernels for 0% -> 0%
where the time goes in v1:
time: 58.2 us; the launch traced here: 58 us
  Pallas kernels  56.4 us (97%)
  local copies, waits for them, and re-layouts  0.88 us (2%)
  between operations  0.68 us (1%)
    pallas_call x1, Pallas kernels, layer(): pl.pallas_call(functools.partial(kernel, sizes, distance), out_shape=jax....  56.4 us

profile of v1, /device:TPU:0, one launch (start us, length us, event | category | flops | bytes accessed | tf_op | source)
XLA Modules:
  0.0 58.0 jit_solution(17826027686976030413)
XLA Ops:
  0.7 56.4 %conditional.1 = (bf16[1,12,16,2048]{3,2,1,0:T(8,128)(2,1)S(1)}) conditional(s32[]{:T(128)} %clamp.3, (bf16[1,12,16,1024]{3,2,1,0:T(8,128)(2,1)}, bf16[1,2,12,16,1024]{4,3,2,1,0:T(8,128)(2,1)}, bf16[1,128,2048]{2,1,0:T(8,128)(2,1)}, bf16[1,256,2048]{2,1,0:T(8,128)(2,1)}, bf16[1,1000,256]{2,1,0:T(8,128)(2,1)}, /*index=5*/s32[1]{0:T(128)}, ...), branch_computations={%region_0.1_spmd, %region_1.2_spmd} | conditional | flops 805306368 | bytes 4194312 | solution.py:401
  0.7 56.4 %sublayer_distance_2.1 = bf16[192,2048]{1,0:T(8,128)(2,1)S(1)} custom-call(bf16[1,12,16,1024]{3,2,1,0:T(8,128)(2,1)} %get-tuple-element.44.q_hbm, bf16[1,2,12,16,1024]{4,3,2,1,0:T(8,128)(2,1)} %get-tuple-element.45.kv_hbm, bf16[1,128,2048]{2,1,0:T(8,128)(2,1)} %get-tuple-element.46.o_hbm, bf16[1,256,2048]{2,1,0:T(8,128)(2,1)} %get-tuple-element.47.g_hbm, ...), custom_call_target="tpu_custom_call" | custom-call | flops 805306368 | bytes 4194304 | tf_op jit(solution)/shard_map/cond/branch_1_fun/sublayer_distance_2/pallas_call | solution.py:348
  57.1 0.9 %copy.15 = bf16[1,12,16,2048]{3,2,1,0:T(8,128)(2,1)} copy(bf16[1,12,16,2048]{3,2,1,0:T(8,128)(2,1)S(1)} %get-tuple-element.51) | data formatting | bytes 1572864

commit v2 on v1

--- a/solution.py
+++ b/solution.py
@@ -10,8 +10,8 @@
 
 HDIM = 128
 RADIUS = 3
-CHUNKS = 4
-GROUP = 4
+CHUNKS = 8
+GROUP = 6
 MESH = pl.DeviceIdType.MESH
 F32 = jnp.float32
 BF16 = jnp.bfloat16
@@ -28,8 +28,8 @@
     q_hbm, kv_hbm, o_hbm, g_hbm, t_hbm, label_ref, step_ref,
     out_hbm,
     q_buf, kv_buf, bias, att, o_own, o_peer, w_buf, out_buf, g_buf, t_buf,
-    pack_out, pack_in, reply_out, reply_in, gates,
-    local_sem, out_sem, gossip_send, gossip_recv, w_up, w_down, w_side, w_recv,
+    pack_out, pack_in, reply_out, reply_in, gates, gate_sum, mate_out,
+    local_sem, out_sem, gossip_send, gossip_recv, w_send, w_side, w_recv, att_send, att_recv, mate_send, mate_recv,
     halo_send, halo_recv, side_send, side_recv, note_send, note_recv, gate_send, gate_recv,
 ):
     n_dp, n_row, n_col = sizes
@@ -48,6 +48,11 @@
     me = r * n_col + c
     ahead, behind = lax.rem(p + distance, n_dp), lax.rem(p + n_dp - distance, n_dp)
     has_up, has_down = r > 0, r < n_row - 1
+    is_outer = (r == 0) | (r == n_row - 1)
+    is_inner = jnp.logical_not(is_outer)
+    mate = r + 1 - 2 * lax.rem(r, 2)
+    onward = 1 + lax.rem(r, 2)
+    tokens = tile_rows * tile_cols
 
     def col_of(step):
         return lax.rem(c + step, n_col)
@@ -102,9 +107,8 @@
         )
 
     def gossip(k):
-        return remote(
-            o_hbm.at[0, :, pl.ds(k * cut, cut)], o_peer.at[k], gossip_send.at[k], gossip_recv.at[k], dp=ahead
-        )
+        columns = pl.ds(k * cut, cut) if isinstance(k, int) else pl.ds(pl.multiple_of(k * cut, cut), cut)
+        return remote(o_hbm.at[0, :, columns], o_peer.at[k], gossip_send.at[k], gossip_recv.at[k], dp=ahead)
 
     gossip(0).start()
     pl.when(has_up)(lambda: halo(0).start())
@@ -132,11 +136,8 @@
         place = w_buf.at[k, rows]
         return remote(place, place, sem, w_recv.at[owner, k], **where)
 
-    def up_copy(row, k):
-        return w_copy(row * n_col + c, k, w_up.at[row, k], row=r - 1)
-
-    def down_copy(row, k):
-        return w_copy(row * n_col + c, k, w_down.at[row, k], row=r + 1)
+    def onward_copy(row, k):
+        return w_copy(row * n_col + c, k, w_send.at[row, k], row=onward)
 
     def side_copy(row, k, step):
         return w_copy(row * n_col + c, k, w_side.at[step - 1, row, k], col=col_of(step))
@@ -147,11 +148,22 @@
 
     def own_chunk(k):
         gossip(k).wait_recv()
-        both = o_own[:, pl.ds(k * cut, cut)].astype(F32) + o_peer[k].astype(F32)
+        columns = pl.ds(pl.multiple_of(k * cut, cut), cut)
+        both = o_own[:, columns].astype(F32) + o_peer[k].astype(F32)
         w_buf[k, pl.ds(pl.multiple_of(me * shard, shard), shard), :] = (0.5 * both).astype(BF16)
-        pl.when(has_up)(lambda: up_copy(r, k).start())
-        pl.when(has_down)(lambda: down_copy(r, k).start())
-        spread(r, k)
+        onward_copy(r, k).start()
+        pl.when(is_inner)(lambda: spread(r, k))
+
+    def hand_on(row, k):
+        onward_copy(row, k).wait_recv()
+        spread(row, k)
+
+    def mate_chunk(k):
+        @pl.when(is_inner)
+        def _():
+            onward_copy(mate, k).wait_recv()
+            onward_copy(mate, k).start()
+            spread(mate, k)
 
     loads[1].wait()
     own_chunk(0)
@@ -208,7 +220,7 @@
     for g in range(tile_rows // GROUP):
         row_here = k_row + (r * tile_rows + g * GROUP - RADIUS)
         seen = near & (row_here >= 0) & (row_here < n_row * tile_rows)
-        bias[g] = seen.astype(F32)
+        bias[g] = jnp.where(seen, 0.0, -1e30)
 
     @pl.when(has_down)
     def _():
@@ -223,6 +235,8 @@
             corner(1, i).start()
 
     own_chunk(2)
+    mate_chunk(0)
+    mate_chunk(1)
 
     answer.wait_recv()
     share = 0.5 * (reply_in[:, pl.ds(0, width)] + against_gate(reply_in[:, pl.ds(width, span)]))
@@ -238,8 +252,8 @@
     for step in range(1, group):
         gate_copy(me, step).start()
 
-    for k in range(3, CHUNKS):
-        own_chunk(k)
+    own_chunk(3)
+    mate_chunk(2)
 
     loads[3].wait()
     loads[4].wait()
@@ -259,35 +273,35 @@
             key = kv_buf[0, near_rows, :, lanes].reshape(n_k, HDIM)
             val = kv_buf[1, near_rows, :, lanes].reshape(n_k, HDIM)
             score = lax.dot_general(query, key, (((1,), (1,)), ((), ())), preferred_element_type=F32)
-            score = jnp.where(bias[g] > 0.5, score, -1e30)
+            score = score + bias[g]
             top = jnp.max(score, axis=1, keepdims=True)
             weight = jnp.exp((score - top) * scale)
             total = jnp.sum(weight, axis=1, keepdims=True)
             mean = jnp.dot(weight.astype(BF16), val, preferred_element_type=F32) / total
             att[pl.ds(g * n_q, n_q), lanes] = mean.astype(BF16)
 
-    def event(e, carry):
-        hop, k = e // CHUNKS + 1, lax.rem(e, CHUNKS)
-
-        @pl.when(r + hop < n_row)
+    pairs = heads // 2
+
+    def att_copy(j):
+        lanes = pl.ds(pl.multiple_of(j * 2 * HDIM, 2 * HDIM), 2 * HDIM)
+        return remote(
+            att.at[pl.ds(0, tokens), lanes], att.at[pl.ds(tokens, tokens), lanes],
+            att_send.at[j], att_recv.at[j], row=mate,
+        )
+
+    def attend_pair(j, carry):
+        @pl.when(j + 4 < CHUNKS)
         def _():
-            row = r + hop
-            up_copy(row, k).wait_recv()
-            pl.when(has_up)(lambda: up_copy(row, k).start())
-            spread(row, k)
-
-        @pl.when((r - hop >= 0) & (hop < n_row))
-        def _():
-            row = r - hop
-            down_copy(row, k).wait_recv()
-            pl.when(has_down)(lambda: down_copy(row, k).start())
-            spread(row, k)
-
-        pl.when(e < heads)(lambda: attend(e))
+            own_chunk(j + 4)
+            mate_chunk(j + 3)
+
+        attend(2 * j)
+        attend(2 * j + 1)
+        pl.when(is_outer)(lambda: att_copy(j).start())
         return carry
 
-    before_last = max(heads, (n_row - 2) * CHUNKS)
-    lax.fori_loop(0, before_last, event, 0)
+    lax.fori_loop(0, pairs, attend_pair, 0)
+    mate_chunk(CHUNKS - 1)
 
     for step in range(1, group):
         owner = lax.rem(me + step, group)
@@ -295,30 +309,68 @@
     gate = gates[0]
     for i in range(1, group):
         gate = gate + gates[i]
+    for k in range(CHUNKS):
+        gate_sum[k] = gate[:, k * cut : (k + 1) * cut]
 
     def out_copy(k):
-        return pltpu.make_async_copy(out_buf.at[k], out_hbm.at[:, pl.ds(k * cut, cut)], out_sem.at[k])
-
-    for k in range(CHUNKS):
-        e = (n_row - 2) * CHUNKS + k
-        if e >= before_last:
-            event(e, 0)
+        return pltpu.make_async_copy(
+            out_buf.at[k], out_hbm.at[:, pl.ds(pl.multiple_of(k * cut, cut), cut)], out_sem.at[k]
+        )
+
+    def mate_copy(k):
+        return remote(
+            mate_out.at[k], out_hbm.at[:, pl.ds(pl.multiple_of(k * cut, cut), cut)],
+            mate_send.at[k], mate_recv.at[k], row=mate,
+        )
+
+    def project(k, carry):
+        hand_on(n_row - 1 - r, k)
+        hand_on(n_row - 1 - mate, k)
         for row in range(n_row):
             for step in range(1, n_col):
                 owner = row * n_col + col_of(step)
                 w_copy(owner, k, w_side.at[step - 1, row, k], col=col_of(step)).wait_recv()
         product = jnp.dot(att[...], w_buf[k], preferred_element_type=F32)
-        out_buf[k] = (gate[:, k * cut : (k + 1) * cut] * product).astype(BF16)
+        product = (gate_sum[k] * product).astype(BF16)
+        mate_out[k] = product[tokens:]
+        mate_copy(k).start()
+        out_buf[k] = product[:tokens]
         out_copy(k).start()
-
-    for k in range(CHUNKS):
-        out_copy(k).wait()
+        return carry
+
+    @pl.when(is_inner)
+    def _():
+        for j in range(pairs):
+            att_copy(j).wait_recv()
+        lax.fori_loop(0, CHUNKS, project, 0)
+
+    @pl.when(is_outer)
+    def _():
+        for k in range(CHUNKS):
+            mate_copy(k).wait_recv()
+
+    def sent(k, carry):
         gossip(k).wait_send()
-        for row in range(n_row):
-            pl.when(has_up & (r <= row))(lambda row=row, k=k: up_copy(row, k).wait_send())
-            pl.when(has_down & (r >= row))(lambda row=row, k=k: down_copy(row, k).wait_send())
-            for step in range(1, n_col):
-                side_copy(row, k, step).wait_send()
+        onward_copy(r, k).wait_send()
+
+        @pl.when(is_inner)
+        def _():
+            out_copy(k).wait()
+            mate_copy(k).wait_send()
+            onward_copy(mate, k).wait_send()
+            for row in range(n_row):
+                for step in range(1, n_col):
+                    side_copy(row, k, step).wait_send()
+
+        return carry
+
+    lax.fori_loop(0, CHUNKS, sent, 0)
+
+    @pl.when(is_outer)
+    def _():
+        for j in range(pairs):
+            att_copy(j).wait_send()
+
     pl.when(has_up)(lambda: halo(0).wait_send())
     pl.when(has_down)(lambda: halo(1).wait_send())
     for i in range(len(sides)):
@@ -354,7 +406,7 @@
             pltpu.VMEM((tile_rows, tile_cols, inner), BF16),
             pltpu.VMEM((2, tile_rows + 2 * RADIUS, wide, inner), BF16),
             pltpu.VMEM((tile_rows // GROUP, n_q, n_k), F32),
-            pltpu.VMEM((tokens, inner), BF16),
+            pltpu.VMEM((2 * tokens, inner), BF16),
             pltpu.VMEM((shard, width), BF16),
             pltpu.VMEM((CHUNKS, shard, cut), BF16),
             pltpu.VMEM((CHUNKS, group * shard, cut), BF16),
@@ -366,14 +418,19 @@
             pltpu.VMEM((1, width + slot), F32),
             pltpu.VMEM((1, width + slot), F32),
             pltpu.VMEM((group, 1, width), F32),
+            pltpu.VMEM((CHUNKS, 1, cut), F32),
+            pltpu.VMEM((CHUNKS, tokens, cut), BF16),
             dma((5,)),
             dma((CHUNKS,)),
             dma((CHUNKS,)),
             dma((CHUNKS,)),
             dma((n_row, CHUNKS)),
-            dma((n_row, CHUNKS)),
             dma((n_col - 1, n_row, CHUNKS)),
             dma((group, CHUNKS)),
+            dma((inner // HDIM // 2,)),
+            dma((inner // HDIM // 2,)),
+            dma((CHUNKS,)),
+            dma((CHUNKS,)),
             dma((2,)),
             dma((2,)),
             dma((3, n_side)),

time: 58.2 us -> 65.2 us (1.12)
  Pallas kernels: 56.4 us -> 63.5 us
    pallas_call x1, Pallas kernels: 56.4 us -> 63.5 us  [layer(): pl.pallas_call(functools.partial(kernel, sizes, distance), out_shape=jax....]
where the time goes in v2:
time: 65.2 us; the launch traced here: 65.1 us
  Pallas kernels  63.5 us (97%)
  local copies, waits for them, and re-layouts  0.88 us (1%)
  between operations  0.68 us (1%)
    pallas_call x1, Pallas kernels, layer(): pl.pallas_call(functools.partial(kernel, sizes, distance), out_shape=jax....  63.5 us

profile of v2, /device:TPU:0, one launch (start us, length us, event | category | flops | bytes accessed | tf_op | source)
XLA Modules:
  0.0 65.1 jit_solution(3959561388457785923)
XLA Ops:
  0.7 63.5 %conditional.1 = (bf16[1,12,16,2048]{3,2,1,0:T(8,128)(2,1)S(1)}) conditional(s32[]{:T(128)} %clamp.3, (bf16[1,12,16,1024]{3,2,1,0:T(8,128)(2,1)}, bf16[1,2,12,16,1024]{4,3,2,1,0:T(8,128)(2,1)}, bf16[1,128,2048]{2,1,0:T(8,128)(2,1)}, bf16[1,256,2048]{2,1,0:T(8,128)(2,1)}, bf16[1,1000,256]{2,1,0:T(8,128)(2,1)}, /*index=5*/s32[1]{0:T(128)}, ...), branch_computations={%region_0.1_spmd, %region_1.2_spmd} | conditional | flops 805306368 | bytes 4194312 | solution.py:458
  0.7 63.5 %sublayer_distance_2.1 = bf16[192,2048]{1,0:T(8,128)(2,1)S(1)} custom-call(bf16[1,12,16,1024]{3,2,1,0:T(8,128)(2,1)} %get-tuple-element.44.q_hbm, bf16[1,2,12,16,1024]{4,3,2,1,0:T(8,128)(2,1)} %get-tuple-element.45.kv_hbm, bf16[1,128,2048]{2,1,0:T(8,128)(2,1)} %get-tuple-element.46.o_hbm, bf16[1,256,2048]{2,1,0:T(8,128)(2,1)} %get-tuple-element.47.g_hbm, ...), custom_call_target="tpu_custom_call" | custom-call | flops 805306368 | bytes 4194304 | tf_op jit(solution)/shard_map/cond/branch_1_fun/sublayer_distance_2/pallas_call | solution.py:400
  64.2 0.9 %copy.15 = bf16[1,12,16,2048]{3,2,1,0:T(8,128)(2,1)} copy(bf16[1,12,16,2048]{3,2,1,0:T(8,128)(2,1)S(1)} %get-tuple-element.51) | data formatting | bytes 1572864

commit v3 on v2

--- a/solution.py
+++ b/solution.py
@@ -11,6 +11,7 @@
 HDIM = 128
 RADIUS = 3
 CHUNKS = 8
+AHEAD = 2
 GROUP = 6
 MESH = pl.DeviceIdType.MESH
 F32 = jnp.float32
@@ -80,44 +81,6 @@
     if (2 * distance) % n_dp:
         pl.semaphore_signal(barrier, inc=1, device_id={"dp": behind}, device_id_type=MESH)
         greeted += 1
-    pl.semaphore_wait(barrier, greeted)
-
-    def halo(which):
-        first, place = ((0, tile_rows + RADIUS), (tile_rows - RADIUS, 0))[which]
-        return remote(
-            kv_hbm.at[0, :, pl.ds(first, RADIUS)],
-            kv_buf.at[:, pl.ds(place, RADIUS), pl.ds(0, tile_cols)],
-            halo_send.at[which], halo_recv.at[which], row=(r - 1, r + 1)[which],
-        )
-
-    def side(i):
-        return remote(
-            kv_hbm.at[0],
-            kv_buf.at[:, pl.ds(RADIUS, tile_rows), pl.ds((i + 1) * tile_cols, tile_cols)],
-            side_send.at[0, i], side_recv.at[0, i], col=col_of(sides[i]),
-        )
-
-    def corner(which, i):
-        place = (tile_rows + RADIUS, 0)[which]
-        rows = pl.ds(place, RADIUS)
-        return remote(
-            kv_buf.at[:, rows, pl.ds(0, tile_cols)],
-            kv_buf.at[:, rows, pl.ds((i + 1) * tile_cols, tile_cols)],
-            side_send.at[1 + which, i], side_recv.at[1 + which, i], col=col_of(sides[i]),
-        )
-
-    def gossip(k):
-        columns = pl.ds(k * cut, cut) if isinstance(k, int) else pl.ds(pl.multiple_of(k * cut, cut), cut)
-        return remote(o_hbm.at[0, :, columns], o_peer.at[k], gossip_send.at[k], gossip_recv.at[k], dp=ahead)
-
-    gossip(0).start()
-    pl.when(has_up)(lambda: halo(0).start())
-    pl.when(has_down)(lambda: halo(1).start())
-    for k in range(1, CHUNKS):
-        gossip(k).start()
-    for i in range(len(sides)):
-        side(i).start()
-
     def class_row(label):
         rows = lax.broadcasted_iota(jnp.int32, (classes, span), 0).astype(F32)
         table = t_buf[...].astype(F32)
@@ -128,67 +91,44 @@
     pack_out[:, pl.ds(0, span)] = label_here
     pack_out[:, pl.ds(slot, span)] = jnp.full((1, span), step_ref[0], jnp.int32).astype(F32)
     pack_out[:, pl.ds(2 * slot, span)] = class_row(label_here)
+    pl.semaphore_wait(barrier, greeted)
+
+    def halo(which):
+        first, place = ((0, tile_rows + RADIUS), (tile_rows - RADIUS, 0))[which]
+        return remote(
+            kv_hbm.at[0, :, pl.ds(first, RADIUS)],
+            kv_buf.at[:, pl.ds(place, RADIUS), pl.ds(0, tile_cols)],
+            halo_send.at[which], halo_recv.at[which], row=(r - 1, r + 1)[which],
+        )
+
+    def side(i):
+        return remote(
+            kv_hbm.at[0],
+            kv_buf.at[:, pl.ds(RADIUS, tile_rows), pl.ds((i + 1) * tile_cols, tile_cols)],
+            side_send.at[0, i], side_recv.at[0, i], col=col_of(sides[i]),
+        )
+
+    def corner(which, i):
+        place = (tile_rows + RADIUS, 0)[which]
+        rows = pl.ds(place, RADIUS)
+        return remote(
+            kv_buf.at[:, rows, pl.ds(0, tile_cols)],
+            kv_buf.at[:, rows, pl.ds((i + 1) * tile_cols, tile_cols)],
+            side_send.at[1 + which, i], side_recv.at[1 + which, i], col=col_of(sides[i]),
+        )
+
+    def gossip(k):
+        columns = pl.ds(k * cut, cut) if isinstance(k, int) else pl.ds(pl.multiple_of(k * cut, cut), cut)
+        return remote(o_hbm.at[0, :, columns], o_peer.at[k], gossip_send.at[k], gossip_recv.at[k], dp=ahead)
+
     ask = remote(pack_out, pack_in, note_send.at[0], note_recv.at[0], dp=behind)
     ask.start()
-
-    def w_copy(owner, k, sem, **where):
-        rows = pl.ds(pl.multiple_of(owner * shard, shard), shard)
-        place = w_buf.at[k, rows]
-        return remote(place, place, sem, w_recv.at[owner, k], **where)
-
-    def onward_copy(row, k):
-        return w_copy(row * n_col + c, k, w_send.at[row, k], row=onward)
-
-    def side_copy(row, k, step):
-        return w_copy(row * n_col + c, k, w_side.at[step - 1, row, k], col=col_of(step))
-
-    def spread(row, k):
-        for step in range(1, n_col):
-            side_copy(row, k, step).start()
-
-    def own_chunk(k):
-        gossip(k).wait_recv()
-        columns = pl.ds(pl.multiple_of(k * cut, cut), cut)
-        both = o_own[:, columns].astype(F32) + o_peer[k].astype(F32)
-        w_buf[k, pl.ds(pl.multiple_of(me * shard, shard), shard), :] = (0.5 * both).astype(BF16)
-        onward_copy(r, k).start()
-        pl.when(is_inner)(lambda: spread(r, k))
-
-    def hand_on(row, k):
-        onward_copy(row, k).wait_recv()
-        spread(row, k)
-
-    def mate_chunk(k):
-        @pl.when(is_inner)
-        def _():
-            onward_copy(mate, k).wait_recv()
-            onward_copy(mate, k).start()
-            spread(mate, k)
-
-    loads[1].wait()
-    own_chunk(0)
-
-    def against_gate(cond):
-        tall = jnp.broadcast_to(cond, (16, span)).astype(BF16)
-        return jnp.dot(tall, g_buf[...], preferred_element_type=F32)[0:1]
-
-    half = width // 2
-    position = me * span + lax.broadcasted_iota(jnp.int32, (1, span), 1)
-    freq_index = jnp.where(position < half, position, position - half).astype(F32)
-    frequency = jnp.exp(-math.log(10000.0) * freq_index / half)
-    ask.wait_recv()
-    mixed_row = 0.5 * (pack_in[:, pl.ds(2 * slot, span)] + class_row(pack_in[:, pl.ds(0, span)]))
-    angle = pack_in[:, pl.ds(slot, span)] * frequency
-    embed = jnp.where(position < half, jnp.cos(angle), jnp.sin(angle))
-    value = mixed_row.astype(BF16).astype(F32) + embed
-    cond = (value / (1.0 + jnp.exp(-value))).astype(BF16).astype(F32)
-    loads[2].wait()
-    reply_out[:, pl.ds(0, width)] = against_gate(cond)
-    reply_out[:, pl.ds(width, span)] = cond
-    answer = remote(reply_out, reply_in, note_send.at[1], note_recv.at[1], dp=ahead)
-    answer.start()
-
-    own_chunk(1)
+    for k in range(AHEAD):
+        gossip(k).start()
+    pl.when(has_up)(lambda: halo(0).start())
+    pl.when(has_down)(lambda: halo(1).start())
+    for i in range(len(sides)):
+        side(i).start()
 
     edge = jnp.zeros((2, RADIUS, wide, inner), BF16)
 
@@ -222,6 +162,52 @@
         seen = near & (row_here >= 0) & (row_here < n_row * tile_rows)
         bias[g] = jnp.where(seen, 0.0, -1e30)
 
+    def w_copy(owner, k, sem, **where):
+        rows = pl.ds(pl.multiple_of(owner * shard, shard), shard)
+        place = w_buf.at[k, rows]
+        return remote(place, place, sem, w_recv.at[owner, k], **where)
+
+    def onward_copy(row, k):
+        return w_copy(row * n_col + c, k, w_send.at[row, k], row=onward)
+
+    def side_copy(row, k, step):
+        return w_copy(row * n_col + c, k, w_side.at[step - 1, row, k], col=col_of(step))
+
+    def spread(row, k):
+        for step in range(1, n_col):
+            side_copy(row, k, step).start()
+
+    def own_chunk(k):
+        gossip(k).wait_recv()
+        gossip(k).wait_send()
+
+        @pl.when(k + AHEAD < CHUNKS)
+        def _():
+            gossip(k + AHEAD).start()
+
+        columns = pl.ds(pl.multiple_of(k * cut, cut), cut)
+        both = o_own[:, columns].astype(F32) + o_peer[k].astype(F32)
+        w_buf[k, pl.ds(pl.multiple_of(me * shard, shard), shard), :] = (0.5 * both).astype(BF16)
+        onward_copy(r, k).start()
+        pl.when(is_inner)(lambda: spread(r, k))
+
+    def hand_on(row, k):
+        onward_copy(row, k).wait_recv()
+        spread(row, k)
+
+    def mate_chunk(k):
+        @pl.when(is_inner)
+        def _():
+            onward_copy(mate, k).wait_recv()
+            onward_copy(mate, k).start()
+            spread(mate, k)
+
+    loads[1].wait()
+    own_chunk(0)
+
+    own_chunk(1)
+    mate_chunk(0)
+
     @pl.when(has_down)
     def _():
         halo(0).wait_recv()
@@ -234,8 +220,28 @@
         for i in range(len(sides)):
             corner(1, i).start()
 
+    def against_gate(cond):
+        tall = jnp.broadcast_to(cond, (16, span)).astype(BF16)
+        return jnp.dot(tall, g_buf[...], preferred_element_type=F32)[0:1]
+
+    half = width // 2
+    position = me * span + lax.broadcasted_iota(jnp.int32, (1, span), 1)
+    freq_index = jnp.where(position < half, position, position - half).astype(F32)
+    frequency = jnp.exp(-math.log(10000.0) * freq_index / half)
+    ask.wait_recv()
+    mixed_row = 0.5 * (pack_in[:, pl.ds(2 * slot, span)] + class_row(pack_in[:, pl.ds(0, span)]))
+    angle = pack_in[:, pl.ds(slot, span)] * frequency
+    embed = jnp.where(position < half, jnp.cos(angle), jnp.sin(angle))
+    value = mixed_row.astype(BF16).astype(F32) + embed
+    cond = (value / (1.0 + jnp.exp(-value))).astype(BF16).astype(F32)
+    loads[2].wait()
+    reply_out[:, pl.ds(0, width)] = against_gate(cond)
+    reply_out[:, pl.ds(width, span)] = cond
+    answer = remote(reply_out, reply_in, note_send.at[1], note_recv.at[1], dp=ahead)
+    answer.start()
+
+
     own_chunk(2)
-    mate_chunk(0)
     mate_chunk(1)
 
     answer.wait_recv()
@@ -282,6 +288,12 @@
 
     pairs = heads // 2
 
+    def other_half(k):
+        @pl.when(is_inner)
+        def _():
+            hand_on(n_row - 1 - r, k)
+            hand_on(n_row - 1 - mate, k)
+
     def att_copy(j):
         lanes = pl.ds(pl.multiple_of(j * 2 * HDIM, 2 * HDIM), 2 * HDIM)
         return remote(
@@ -295,6 +307,7 @@
             own_chunk(j + 4)
             mate_chunk(j + 3)
 
+        pl.when(j > 0)(lambda: other_half(j - 1))
         attend(2 * j)
         attend(2 * j + 1)
         pl.when(is_outer)(lambda: att_copy(j).start())
@@ -302,6 +315,7 @@
 
     lax.fori_loop(0, pairs, attend_pair, 0)
     mate_chunk(CHUNKS - 1)
+    other_half(pairs - 1)
 
     for step in range(1, group):
         owner = lax.rem(me + step, group)
@@ -324,8 +338,7 @@
         )
 
     def project(k, carry):
-        hand_on(n_row - 1 - r, k)
-        hand_on(n_row - 1 - mate, k)
+        pl.when((k + 1 >= pairs) & (k + 1 < CHUNKS))(lambda: other_half(k + 1))
         for row in range(n_row):
             for step in range(1, n_col):
                 owner = row * n_col + col_of(step)
@@ -350,7 +363,6 @@
             mate_copy(k).wait_recv()
 
     def sent(k, carry):
-        gossip(k).wait_send()
         onward_copy(r, k).wait_send()
 
         @pl.when(is_inner)

time: 65.2 us -> 56.2 us (0.86)
  Pallas kernels: 63.5 us -> 53.9 us
    pallas_call x1, Pallas kernels: 63.5 us -> 53.9 us  [layer(): pl.pallas_call(functools.partial(kernel, sizes, distance), out_shape=jax....]
where the time goes in v3:
time: 56.2 us; the launch traced here: 55.5 us
  Pallas kernels  53.9 us (96%)
  local copies, waits for them, and re-layouts  0.88 us (2%)
  between operations  0.68 us (1%)
    pallas_call x1, Pallas kernels, layer(): pl.pallas_call(functools.partial(kernel, sizes, distance), out_shape=jax....  53.9 us

profile of v3, /device:TPU:0, one launch (start us, length us, event | category | flops | bytes accessed | tf_op | source)
XLA Modules:
  0.0 55.5 jit_solution(17769679760526097104)
XLA Ops:
  0.7 53.9 %conditional.1 = (bf16[1,12,16,2048]{3,2,1,0:T(8,128)(2,1)S(1)}) conditional(s32[]{:T(128)} %clamp.3, (bf16[1,12,16,1024]{3,2,1,0:T(8,128)(2,1)}, bf16[1,2,12,16,1024]{4,3,2,1,0:T(8,128)(2,1)}, bf16[1,128,2048]{2,1,0:T(8,128)(2,1)}, bf16[1,256,2048]{2,1,0:T(8,128)(2,1)}, bf16[1,1000,256]{2,1,0:T(8,128)(2,1)}, /*index=5*/s32[1]{0:T(128)}, ...), branch_computations={%region_0.1_spmd, %region_1.2_spmd} | conditional | flops 805306368 | bytes 4194312 | solution.py:470
  0.7 53.9 %sublayer_distance_2.1 = bf16[192,2048]{1,0:T(8,128)(2,1)S(1)} custom-call(bf16[1,12,16,1024]{3,2,1,0:T(8,128)(2,1)} %get-tuple-element.44.q_hbm, bf16[1,2,12,16,1024]{4,3,2,1,0:T(8,128)(2,1)} %get-tuple-element.45.kv_hbm, bf16[1,128,2048]{2,1,0:T(8,128)(2,1)} %get-tuple-element.46.o_hbm, bf16[1,256,2048]{2,1,0:T(8,128)(2,1)} %get-tuple-element.47.g_hbm, ...), custom_call_target="tpu_custom_call" | custom-call | flops 805306368 | bytes 4194304 | tf_op jit(solution)/shard_map/cond/branch_1_fun/sublayer_distance_2/pallas_call | solution.py:412
  54.6 0.9 %copy.15 = bf16[1,12,16,2048]{3,2,1,0:T(8,128)(2,1)} copy(bf16[1,12,16,2048]{3,2,1,0:T(8,128)(2,1)S(1)} %get-tuple-element.51) | data formatting | bytes 1572864

commit v4 on v3

--- a/solution.py
+++ b/solution.py
@@ -12,6 +12,7 @@
 RADIUS = 3
 CHUNKS = 8
 AHEAD = 2
+OUTER = 2
 GROUP = 6
 MESH = pl.DeviceIdType.MESH
 F32 = jnp.float32
@@ -30,7 +31,7 @@
     out_hbm,
     q_buf, kv_buf, bias, att, o_own, o_peer, w_buf, out_buf, g_buf, t_buf,
     pack_out, pack_in, reply_out, reply_in, gates, gate_sum, mate_out,
-    local_sem, out_sem, gossip_send, gossip_recv, w_send, w_side, w_recv, att_send, att_recv, mate_send, mate_recv,
+    local_sem, out_sem, gossip_send, gossip_recv, w_send, w_back, w_side, w_recv, att_send, att_recv, mate_send, mate_recv,
     halo_send, halo_recv, side_send, side_recv, note_send, note_recv, gate_send, gate_recv,
 ):
     n_dp, n_row, n_col = sizes
@@ -170,6 +171,9 @@
     def onward_copy(row, k):
         return w_copy(row * n_col + c, k, w_send.at[row, k], row=onward)
 
+    def back_copy(row, k):
+        return w_copy(row * n_col + c, k, w_back.at[row, k], row=mate)
+
     def side_copy(row, k, step):
         return w_copy(row * n_col + c, k, w_side.at[step - 1, row, k], col=col_of(step))
 
@@ -189,7 +193,8 @@
         both = o_own[:, columns].astype(F32) + o_peer[k].astype(F32)
         w_buf[k, pl.ds(pl.multiple_of(me * shard, shard), shard), :] = (0.5 * both).astype(BF16)
         onward_copy(r, k).start()
-        pl.when(is_inner)(lambda: spread(r, k))
+        pl.when(is_inner | (k < OUTER))(lambda: spread(r, k))
+        pl.when(is_inner & (k < OUTER))(lambda: back_copy(r, k).start())
 
     def hand_on(row, k):
         onward_copy(row, k).wait_recv()
@@ -270,29 +275,41 @@
 
     scale = 1.0 / math.sqrt(HDIM)
 
-    def attend(head):
-        lanes = pl.ds(pl.multiple_of(head * HDIM, HDIM), HDIM)
-        for g in range(tile_rows // GROUP):
-            rows = pl.ds(g * GROUP, GROUP)
-            near_rows = pl.ds(g * GROUP, GROUP + 2 * RADIUS)
-            query = q_buf[rows, :, lanes].reshape(n_q, HDIM)
-            key = kv_buf[0, near_rows, :, lanes].reshape(n_k, HDIM)
-            val = kv_buf[1, near_rows, :, lanes].reshape(n_k, HDIM)
-            score = lax.dot_general(query, key, (((1,), (1,)), ((), ())), preferred_element_type=F32)
-            score = score + bias[g]
-            top = jnp.max(score, axis=1, keepdims=True)
-            weight = jnp.exp((score - top) * scale)
-            total = jnp.sum(weight, axis=1, keepdims=True)
-            mean = jnp.dot(weight.astype(BF16), val, preferred_element_type=F32) / total
-            att[pl.ds(g * n_q, n_q), lanes] = mean.astype(BF16)
+    def attend(first):
+        parts = [(first + i, g) for i in range(2) for g in range(tile_rows // GROUP)]
+
+        def lanes(head):
+            return pl.ds(pl.multiple_of(head * HDIM, HDIM), HDIM)
+
+        def near_rows(which, head, g):
+            return kv_buf[which, pl.ds(g * GROUP, GROUP + 2 * RADIUS), :, lanes(head)].reshape(n_k, HDIM)
+
+        scores = []
+        for head, g in parts:
+            query = q_buf[pl.ds(g * GROUP, GROUP), :, lanes(head)].reshape(n_q, HDIM)
+            score = lax.dot_general(
+                query, near_rows(0, head, g), (((1,), (1,)), ((), ())), preferred_element_type=F32
+            )
+            scores.append(score + bias[g])
+        tops = [jnp.max(score, axis=1, keepdims=True) for score in scores]
+        weights = [jnp.exp((score - top) * scale) for score, top in zip(scores, tops)]
+        totals = [jnp.sum(weight, axis=1, keepdims=True) for weight in weights]
+        sums = [
+            jnp.dot(weight.astype(BF16), near_rows(1, head, g), preferred_element_type=F32)
+            for weight, (head, g) in zip(weights, parts)
+        ]
+        means = [(part / total).astype(BF16) for part, total in zip(sums, totals)]
+        for mean, (head, g) in zip(means, parts):
+            att[pl.ds(g * n_q, n_q), lanes(head)] = mean
 
     pairs = heads // 2
 
     def other_half(k):
         @pl.when(is_inner)
         def _():
-            hand_on(n_row - 1 - r, k)
-            hand_on(n_row - 1 - mate, k)
+            for row in (n_row - 1 - r, n_row - 1 - mate):
+                hand_on(row, k)
+                pl.when(k < OUTER)(lambda row=row: back_copy(row, k).start())
 
     def att_copy(j):
         lanes = pl.ds(pl.multiple_of(j * 2 * HDIM, 2 * HDIM), 2 * HDIM)
@@ -309,7 +326,6 @@
 
         pl.when(j > 0)(lambda: other_half(j - 1))
         attend(2 * j)
-        attend(2 * j + 1)
         pl.when(is_outer)(lambda: att_copy(j).start())
         return carry
 
@@ -337,42 +353,72 @@
             mate_send.at[k], mate_recv.at[k], row=mate,
         )
 
-    def project(k, carry):
-        pl.when((k + 1 >= pairs) & (k + 1 < CHUNKS))(lambda: other_half(k + 1))
+    def from_side(k):
         for row in range(n_row):
             for step in range(1, n_col):
                 owner = row * n_col + col_of(step)
                 w_copy(owner, k, w_side.at[step - 1, row, k], col=col_of(step)).wait_recv()
-        product = jnp.dot(att[...], w_buf[k], preferred_element_type=F32)
-        product = (gate_sum[k] * product).astype(BF16)
-        mate_out[k] = product[tokens:]
-        mate_copy(k).start()
-        out_buf[k] = product[:tokens]
+
+    def rows_of(start, k):
+        product = jnp.dot(att[pl.ds(start, tokens)], w_buf[k], preferred_element_type=F32)
+        return (gate_sum[k] * product).astype(BF16)
+
+    def own_rows(k):
+        out_buf[k] = rows_of(0, k)
         out_copy(k).start()
+
+    def project(k, carry):
+        pl.when((k + 1 >= pairs) & (k + 1 < CHUNKS))(lambda: other_half(k + 1))
+        from_side(k)
+
+        @pl.when(k == OUTER)
+        def _():
+            for j in range(pairs):
+                att_copy(j).wait_recv()
+
+        @pl.when(k >= OUTER)
+        def _():
+            mate_out[k] = rows_of(tokens, k)
+            mate_copy(k).start()
+
+        own_rows(k)
         return carry
 
     @pl.when(is_inner)
     def _():
-        for j in range(pairs):
-            att_copy(j).wait_recv()
         lax.fori_loop(0, CHUNKS, project, 0)
 
     @pl.when(is_outer)
     def _():
-        for k in range(CHUNKS):
+        for k in range(OUTER):
+            for row in (mate, n_row - 1 - mate, n_row - 1 - r):
+                back_copy(row, k).wait_recv()
+                spread(row, k)
+        for k in range(OUTER):
+            from_side(k)
+            own_rows(k)
+        for k in range(OUTER, CHUNKS):
             mate_copy(k).wait_recv()
 
     def sent(k, carry):
         onward_copy(r, k).wait_send()
 
-        @pl.when(is_inner)
+        @pl.when(is_inner | (k < OUTER))
         def _():
             out_copy(k).wait()
-            mate_copy(k).wait_send()
-            onward_copy(mate, k).wait_send()
             for row in range(n_row):
                 for step in range(1, n_col):
                     side_copy(row, k, step).wait_send()
+
+        @pl.when(is_inner)
+        def _():
+            onward_copy(mate, k).wait_send()
+            pl.when(k >= OUTER)(lambda: mate_copy(k).wait_send())
+
+            @pl.when(k < OUTER)
+            def _():
+                for row in (r, n_row - 1 - r, n_row - 1 - mate):
+                    back_copy(row, k).wait_send()
 
         return carry
 
@@ -437,6 +483,7 @@
             dma((CHUNKS,)),
             dma((CHUNKS,)),
             dma((n_row, CHUNKS)),
+            dma((n_row, CHUNKS)),
             dma((n_col - 1, n_row, CHUNKS)),
             dma((group, CHUNKS)),
             dma((inner // HDIM // 2,)),

time: 56.2 us -> 53.6 us (0.954); the launches traced: 55.5 us -> 53.5 us
  Pallas kernels: 53.9 us -> 51.9 us
    pallas_call x1, Pallas kernels: 53.9 us -> 51.9 us  [layer(): pl.pallas_call(functools.partial(kernel, sizes, distance), out_shape=jax....]
where the time goes in v4:
time: 53.6 us; the launch traced here: 53.5 us
  Pallas kernels  51.9 us (97%)
  local copies, waits for them, and re-layouts  0.88 us (2%)
  between operations  0.68 us (1%)
    pallas_call x1, Pallas kernels, layer(): pl.pallas_call(functools.partial(kernel, sizes, distance), out_shape=jax....  51.9 us

profile of v4, /device:TPU:0, one launch (start us, length us, event | category | flops | bytes accessed | tf_op | source)
XLA Modules:
  0.0 53.5 jit_solution(3387172909456674676)
XLA Ops:
  0.7 51.9 %conditional.1 = (bf16[1,12,16,2048]{3,2,1,0:T(8,128)(2,1)S(1)}) conditional(s32[]{:T(128)} %clamp.3, (bf16[1,12,16,1024]{3,2,1,0:T(8,128)(2,1)}, bf16[1,2,12,16,1024]{4,3,2,1,0:T(8,128)(2,1)}, bf16[1,128,2048]{2,1,0:T(8,128)(2,1)}, bf16[1,256,2048]{2,1,0:T(8,128)(2,1)}, bf16[1,1000,256]{2,1,0:T(8,128)(2,1)}, /*index=5*/s32[1]{0:T(128)}, ...), branch_computations={%region_0.1_spmd, %region_1.2_spmd} | conditional | flops 805306368 | bytes 4194312 | solution.py:517
  0.7 51.9 %sublayer_distance_1.1 = bf16[192,2048]{1,0:T(8,128)(2,1)S(1)} custom-call(bf16[1,12,16,1024]{3,2,1,0:T(8,128)(2,1)} %get-tuple-element.37.q_hbm, bf16[1,2,12,16,1024]{4,3,2,1,0:T(8,128)(2,1)} %get-tuple-element.38.kv_hbm, bf16[1,128,2048]{2,1,0:T(8,128)(2,1)} %get-tuple-element.39.o_hbm, bf16[1,256,2048]{2,1,0:T(8,128)(2,1)} %get-tuple-element.40.g_hbm, ...), custom_call_target="tpu_custom_call" | custom-call | flops 805306368 | bytes 4194304 | tf_op jit(solution)/shard_map/cond/branch_0_fun/sublayer_distance_1/pallas_call | solution.py:458
  52.6 0.9 %copy.15 = bf16[1,12,16,2048]{3,2,1,0:T(8,128)(2,1)} copy(bf16[1,12,16,2048]{3,2,1,0:T(8,128)(2,1)S(1)} %get-tuple-element.51) | data formatting | bytes 1572864

commit v5 on v4

--- a/solution.py
+++ b/solution.py
@@ -13,7 +13,6 @@
 CHUNKS = 8
 AHEAD = 2
 OUTER = 2
-GROUP = 6
 MESH = pl.DeviceIdType.MESH
 F32 = jnp.float32
 BF16 = jnp.bfloat16
@@ -29,7 +28,7 @@
     sizes, distance,
     q_hbm, kv_hbm, o_hbm, g_hbm, t_hbm, label_ref, step_ref,
     out_hbm,
-    q_buf, kv_buf, bias, att, o_own, o_peer, w_buf, out_buf, g_buf, t_buf,
+    q_buf, kv_buf, bias_mid, bias_edge, att, o_own, o_peer, w_buf, out_buf, g_buf, t_buf,
     pack_out, pack_in, reply_out, reply_in, gates, gate_sum, mate_out,
     local_sem, out_sem, gossip_send, gossip_recv, w_send, w_back, w_side, w_recv, att_send, att_recv, mate_send, mate_recv,
     halo_send, halo_recv, side_send, side_recv, note_send, note_recv, gate_send, gate_recv,
@@ -141,27 +140,37 @@
     def _():
         kv_buf[:, pl.ds(tile_rows + RADIUS, RADIUS)] = edge
 
-    n_q, n_k = GROUP * tile_cols, (GROUP + 2 * RADIUS) * wide
     blocks = wide // tile_cols
-    q_index = lax.broadcasted_iota(jnp.int32, (n_q, n_k), 0)
-    k_index = lax.broadcasted_iota(jnp.int32, (n_q, n_k), 1)
-    q_row, q_col = q_index // tile_cols, lax.rem(q_index, tile_cols)
-    k_block = k_index // tile_cols
-    k_row = (k_block * -(-512 // blocks)) // 512
-    k_block = k_block - k_row * blocks
-    k_col = lax.rem(k_index, tile_cols)
-    if n_col == 2:
-        k_shift = jnp.where(k_block == 1, 1 - 2 * c, 0)
-    else:
-        k_shift = jnp.where(k_block == 1, 1, jnp.where(k_block == 2, -1, 0))
-    k_col = k_col + k_shift * tile_cols
-    near = (jnp.abs(k_col - q_col) <= RADIUS) & (k_row >= q_row) & (k_row <= q_row + 2 * RADIUS)
-    k_col = k_col + c * tile_cols
-    near = near & (k_col >= 0) & (k_col < n_col * tile_cols)
-    for g in range(tile_rows // GROUP):
-        row_here = k_row + (r * tile_rows + g * GROUP - RADIUS)
-        seen = near & (row_here >= 0) & (row_here < n_row * tile_rows)
-        bias[g] = jnp.where(seen, 0.0, -1e30)
+    mid_rows = tile_rows - 2 * RADIUS
+
+    def allowed(q_start, q_rows, k_start):
+        extent = (q_rows * tile_cols, tile_rows * wide)
+        q_index = lax.broadcasted_iota(jnp.int32, extent, 0)
+        k_index = lax.broadcasted_iota(jnp.int32, extent, 1)
+        q_row, q_col = q_start + q_index // tile_cols, lax.rem(q_index, tile_cols)
+        k_block = k_index // tile_cols
+        k_row = (k_block * -(-512 // blocks)) // 512
+        k_block = k_block - k_row * blocks
+        k_row = k_row + k_start
+        k_col = lax.rem(k_index, tile_cols)
+        if n_col == 2:
+            k_shift = jnp.where(k_block == 1, 1 - 2 * c, 0)
+        else:
+            k_shift = jnp.where(k_block == 1, 1, jnp.where(k_block == 2, -1, 0))
+        k_col = k_col + k_shift * tile_cols
+        near = (jnp.abs(k_col - q_col) <= RADIUS) & (k_row >= q_row) & (k_row <= q_row + 2 * RADIUS)
+        k_col = k_col + c * tile_cols
+        k_row = k_row + (r * tile_rows - RADIUS)
+        inside = (k_col >= 0) & (k_col < n_col * tile_cols) & (k_row >= 0) & (k_row < n_row * tile_rows)
+        return jnp.where(near & inside, 0.0, -1e30)
+
+    middle = (RADIUS, mid_rows, RADIUS, bias_mid)
+    edges = (
+        (0, RADIUS, 0, bias_edge.at[0]),
+        (tile_rows - RADIUS, RADIUS, 2 * RADIUS, bias_edge.at[1]),
+    )
+    for q_start, q_rows, k_start, mask in (middle,) + edges:
+        mask[...] = allowed(q_start, q_rows, k_start)
 
     def w_copy(owner, k, sem, **where):
         rows = pl.ds(pl.multiple_of(owner * shard, shard), shard)
@@ -207,11 +216,42 @@
             onward_copy(mate, k).start()
             spread(mate, k)
 
+    scale = 1.0 / math.sqrt(HDIM)
+
+    def attend(parts):
+        def lanes(head):
+            return pl.ds(pl.multiple_of(head * HDIM, HDIM), HDIM)
+
+        def near_rows(which, head, k_start):
+            return kv_buf[which, pl.ds(k_start, tile_rows), :, lanes(head)].reshape(tile_rows * wide, HDIM)
+
+        scores = []
+        for head, (q_start, q_rows, k_start, mask) in parts:
+            query = q_buf[pl.ds(q_start, q_rows), :, lanes(head)].reshape(q_rows * tile_cols, HDIM)
+            score = lax.dot_general(
+                query, near_rows(0, head, k_start), (((1,), (1,)), ((), ())), preferred_element_type=F32
+            )
+            scores.append(score + mask[...])
+        tops = [jnp.max(score, axis=1, keepdims=True) for score in scores]
+        weights = [jnp.exp((score - top) * scale) for score, top in zip(scores, tops)]
+        totals = [jnp.sum(weight, axis=1, keepdims=True) for weight in weights]
+        sums = [
+            jnp.dot(weight.astype(BF16), near_rows(1, head, k_start), preferred_element_type=F32)
+            for weight, (head, (_, _, k_start, _)) in zip(weights, parts)
+        ]
+        means = [(part / total).astype(BF16) for part, total in zip(sums, totals)]
+        for mean, (head, (q_start, q_rows, _, _)) in zip(means, parts):
+            att[pl.ds(q_start * tile_cols, q_rows * tile_cols), lanes(head)] = mean
+
     loads[1].wait()
     own_chunk(0)
+    loads[3].wait()
+    loads[4].wait()
+    for i in range(len(sides)):
+        side(i).wait_recv()
 
     own_chunk(1)
-    mate_chunk(0)
+    attend([(head, middle) for head in range(heads // 2)])
 
     @pl.when(has_down)
     def _():
@@ -224,6 +264,12 @@
         halo(1).wait_recv()
         for i in range(len(sides)):
             corner(1, i).start()
+
+    own_chunk(2)
+    mate_chunk(0)
+    attend([(head, middle) for head in range(heads // 2, heads)])
+    own_chunk(3)
+    mate_chunk(1)
 
     def against_gate(cond):
         tall = jnp.broadcast_to(cond, (16, span)).astype(BF16)
@@ -246,12 +292,25 @@
     answer.start()
 
 
-    own_chunk(2)
-    mate_chunk(1)
-
-    answer.wait_recv()
-    share = 0.5 * (reply_in[:, pl.ds(0, width)] + against_gate(reply_in[:, pl.ds(width, span)]))
-    gates[me] = share
+    for i in range(len(sides)):
+        pl.when(has_down)(lambda i=i: corner(0, i).wait_recv())
+        pl.when(has_up)(lambda i=i: corner(1, i).wait_recv())
+
+    pairs = heads // 2
+
+    def other_half(k):
+        @pl.when(is_inner)
+        def _():
+            for row in (n_row - 1 - r, n_row - 1 - mate):
+                hand_on(row, k)
+                pl.when(k < OUTER)(lambda row=row: back_copy(row, k).start())
+
+    def att_copy(j):
+        lanes = pl.ds(pl.multiple_of(j * 2 * HDIM, 2 * HDIM), 2 * HDIM)
+        return remote(
+            att.at[pl.ds(0, tokens), lanes], att.at[pl.ds(tokens, tokens), lanes],
+            att_send.at[j], att_recv.at[j], row=mate,
+        )
 
     def gate_copy(owner, step):
         other = lax.rem(me + step, group)
@@ -260,77 +319,29 @@
             row=other // n_col, col=lax.rem(other, n_col),
         )
 
-    for step in range(1, group):
-        gate_copy(me, step).start()
-
-    own_chunk(3)
-    mate_chunk(2)
-
-    loads[3].wait()
-    loads[4].wait()
-    for i in range(len(sides)):
-        side(i).wait_recv()
-        pl.when(has_down)(lambda i=i: corner(0, i).wait_recv())
-        pl.when(has_up)(lambda i=i: corner(1, i).wait_recv())
-
-    scale = 1.0 / math.sqrt(HDIM)
-
-    def attend(first):
-        parts = [(first + i, g) for i in range(2) for g in range(tile_rows // GROUP)]
-
-        def lanes(head):
-            return pl.ds(pl.multiple_of(head * HDIM, HDIM), HDIM)
-
-        def near_rows(which, head, g):
-            return kv_buf[which, pl.ds(g * GROUP, GROUP + 2 * RADIUS), :, lanes(head)].reshape(n_k, HDIM)
-
-        scores = []
-        for head, g in parts:
-            query = q_buf[pl.ds(g * GROUP, GROUP), :, lanes(head)].reshape(n_q, HDIM)
-            score = lax.dot_general(
-                query, near_rows(0, head, g), (((1,), (1,)), ((), ())), preferred_element_type=F32
-            )
-            scores.append(score + bias[g])
-        tops = [jnp.max(score, axis=1, keepdims=True) for score in scores]
-        weights = [jnp.exp((score - top) * scale) for score, top in zip(scores, tops)]
-        totals = [jnp.sum(weight, axis=1, keepdims=True) for weight in weights]
-        sums = [
-            jnp.dot(weight.astype(BF16), near_rows(1, head, g), preferred_element_type=F32)
-            for weight, (head, g) in zip(weights, parts)
-        ]
-        means = [(part / total).astype(BF16) for part, total in zip(sums, totals)]
-        for mean, (head, g) in zip(means, parts):
-            att[pl.ds(g * n_q, n_q), lanes(head)] = mean
-
-    pairs = heads // 2
-
-    def other_half(k):
-        @pl.when(is_inner)
-        def _():
-            for row in (n_row - 1 - r, n_row - 1 - mate):
-                hand_on(row, k)
-                pl.when(k < OUTER)(lambda row=row: back_copy(row, k).start())
-
-    def att_copy(j):
-        lanes = pl.ds(pl.multiple_of(j * 2 * HDIM, 2 * HDIM), 2 * HDIM)
-        return remote(
-            att.at[pl.ds(0, tokens), lanes], att.at[pl.ds(tokens, tokens), lanes],
-            att_send.at[j], att_recv.at[j], row=mate,
-        )
+    def send_share():
+        answer.wait_recv()
+        share = 0.5 * (reply_in[:, pl.ds(0, width)] + against_gate(reply_in[:, pl.ds(width, span)]))
+        gates[me] = share
+        for step in range(1, group):
+            gate_copy(me, step).start()
 
     def attend_pair(j, carry):
         @pl.when(j + 4 < CHUNKS)
         def _():
             own_chunk(j + 4)
-            mate_chunk(j + 3)
-
-        pl.when(j > 0)(lambda: other_half(j - 1))
-        attend(2 * j)
+            mate_chunk(j + 2)
+
+        pl.when(j == 1)(send_share)
+        pl.when(j > 1)(lambda: other_half(j - 2))
+        attend([(2 * j + i, edge) for i in range(2) for edge in edges])
         pl.when(is_outer)(lambda: att_copy(j).start())
         return carry
 
     lax.fori_loop(0, pairs, attend_pair, 0)
+    mate_chunk(CHUNKS - 2)
     mate_chunk(CHUNKS - 1)
+    other_half(pairs - 2)
     other_half(pairs - 1)
 
     for step in range(1, group):
@@ -359,12 +370,12 @@
                 owner = row * n_col + col_of(step)
                 w_copy(owner, k, w_side.at[step - 1, row, k], col=col_of(step)).wait_recv()
 
-    def rows_of(start, k):
-        product = jnp.dot(att[pl.ds(start, tokens)], w_buf[k], preferred_element_type=F32)
+    def rows_of(count, k):
+        product = jnp.dot(att[pl.ds(0, count)], w_buf[k], preferred_element_type=F32)
         return (gate_sum[k] * product).astype(BF16)
 
     def own_rows(k):
-        out_buf[k] = rows_of(0, k)
+        out_buf[k] = rows_of(tokens, k)
         out_copy(k).start()
 
     def project(k, carry):
@@ -378,10 +389,13 @@
 
         @pl.when(k >= OUTER)
         def _():
-            mate_out[k] = rows_of(tokens, k)
+            both = rows_of(2 * tokens, k)
+            mate_out[k] = both[tokens:]
             mate_copy(k).start()
-
-        own_rows(k)
+            out_buf[k] = both[:tokens]
+            out_copy(k).start()
+
+        pl.when(k < OUTER)(lambda: own_rows(k))
         return carry
 
     @pl.when(is_inner)
@@ -453,7 +467,7 @@
     n_side = 1 if n_col == 2 else 2
     wide = tile_cols * (1 + n_side)
     tokens = tile_rows * tile_cols
-    n_q, n_k = GROUP * tile_cols, (GROUP + 2 * RADIUS) * wide
+    n_k = tile_rows * wide
     dma = pltpu.SemaphoreType.DMA
     return pl.pallas_call(
         functools.partial(kernel, sizes, distance),
@@ -463,7 +477,8 @@
         scratch_shapes=[
             pltpu.VMEM((tile_rows, tile_cols, inner), BF16),
             pltpu.VMEM((2, tile_rows + 2 * RADIUS, wide, inner), BF16),
-            pltpu.VMEM((tile_rows // GROUP, n_q, n_k), F32),
+            pltpu.VMEM(((tile_rows - 2 * RADIUS) * tile_cols, n_k), F32),
+            pltpu.VMEM((2, RADIUS * tile_cols, n_k), F32),
             pltpu.VMEM((2 * tokens, inner), BF16),
             pltpu.VMEM((shard, width), BF16),
             pltpu.VMEM((CHUNKS, shard, cut), BF16),

time: 53.6 us -> 54.2 us (1.011)
  no operation moved by 1% of the time
where the time goes in v5:
time: 54.2 us; the launch traced here: 54 us
  Pallas kernels  52.4 us (97%)
  local copies, waits for them, and re-layouts  0.88 us (2%)
  between operations  0.68 us (1%)
    pallas_call x1, Pallas kernels, layer(): pl.pallas_call(functools.partial(kernel, sizes, distance), out_shape=jax....  52.4 us

profile of v5, /device:TPU:0, one launch (start us, length us, event | category | flops | bytes accessed | tf_op | source)
XLA Modules:
  0.0 54.0 jit_solution(684265075395595433)
XLA Ops:
  0.7 52.4 %conditional.1 = (bf16[1,12,16,2048]{3,2,1,0:T(8,128)(2,1)S(1)}) conditional(s32[]{:T(128)} %clamp.3, (bf16[1,12,16,1024]{3,2,1,0:T(8,128)(2,1)}, bf16[1,2,12,16,1024]{4,3,2,1,0:T(8,128)(2,1)}, bf16[1,128,2048]{2,1,0:T(8,128)(2,1)}, bf16[1,256,2048]{2,1,0:T(8,128)(2,1)}, bf16[1,1000,256]{2,1,0:T(8,128)(2,1)}, /*index=5*/s32[1]{0:T(128)}, ...), branch_computations={%region_0.1_spmd, %region_1.2_spmd} | conditional | flops 805306368 | bytes 4194312 | solution.py:532
  0.7 52.4 %sublayer_distance_1.1 = bf16[192,2048]{1,0:T(8,128)(2,1)S(1)} custom-call(bf16[1,12,16,1024]{3,2,1,0:T(8,128)(2,1)} %get-tuple-element.37.q_hbm, bf16[1,2,12,16,1024]{4,3,2,1,0:T(8,128)(2,1)} %get-tuple-element.38.kv_hbm, bf16[1,128,2048]{2,1,0:T(8,128)(2,1)} %get-tuple-element.39.o_hbm, bf16[1,256,2048]{2,1,0:T(8,128)(2,1)} %get-tuple-element.40.g_hbm, ...), custom_call_target="tpu_custom_call" | custom-call | flops 805306368 | bytes 4194304 | tf_op jit(solution)/shard_map/cond/branch_0_fun/sublayer_distance_1/pallas_call | solution.py:472
  53.1 0.9 %copy.15 = bf16[1,12,16,2048]{3,2,1,0:T(8,128)(2,1)} copy(bf16[1,12,16,2048]{3,2,1,0:T(8,128)(2,1)S(1)} %get-tuple-element.51) | data formatting | bytes 1572864

commit v6 on v5

--- a/solution.py
+++ b/solution.py
@@ -11,8 +11,8 @@
 HDIM = 128
 RADIUS = 3
 CHUNKS = 8
-AHEAD = 2
-OUTER = 2
+AHEAD = 3
+OUTER = 3
 MESH = pl.DeviceIdType.MESH
 F32 = jnp.float32
 BF16 = jnp.bfloat16
@@ -250,8 +250,28 @@
     for i in range(len(sides)):
         side(i).wait_recv()
 
+    att_parts = (
+        (RADIUS * tile_cols, mid_rows * tile_cols),
+        (0, RADIUS * tile_cols),
+        ((tile_rows - RADIUS) * tile_cols, RADIUS * tile_cols),
+    )
+
+    def att_copy(i):
+        start, count = att_parts[i]
+        return remote(
+            att.at[pl.ds(start, count)], att.at[pl.ds(tokens + start, count)],
+            att_send.at[i], att_recv.at[i], row=mate,
+        )
+
+    quarter = heads // 4
+
+    def attend_middle(i):
+        attend([(head, middle) for head in range(i * quarter, (i + 1) * quarter)])
+
     own_chunk(1)
-    attend([(head, middle) for head in range(heads // 2)])
+    attend_middle(0)
+    own_chunk(2)
+    attend_middle(1)
 
     @pl.when(has_down)
     def _():
@@ -265,11 +285,15 @@
         for i in range(len(sides)):
             corner(1, i).start()
 
-    own_chunk(2)
+    own_chunk(3)
     mate_chunk(0)
-    attend([(head, middle) for head in range(heads // 2, heads)])
-    own_chunk(3)
+    attend_middle(2)
+    own_chunk(4)
     mate_chunk(1)
+    attend_middle(3)
+    pl.when(is_outer)(lambda: att_copy(0).start())
+    own_chunk(5)
+    mate_chunk(2)
 
     def against_gate(cond):
         tall = jnp.broadcast_to(cond, (16, span)).astype(BF16)
@@ -305,13 +329,6 @@
                 hand_on(row, k)
                 pl.when(k < OUTER)(lambda row=row: back_copy(row, k).start())
 
-    def att_copy(j):
-        lanes = pl.ds(pl.multiple_of(j * 2 * HDIM, 2 * HDIM), 2 * HDIM)
-        return remote(
-            att.at[pl.ds(0, tokens), lanes], att.at[pl.ds(tokens, tokens), lanes],
-            att_send.at[j], att_recv.at[j], row=mate,
-        )
-
     def gate_copy(owner, step):
         other = lax.rem(me + step, group)
         return remote(
@@ -327,22 +344,25 @@
             gate_copy(me, step).start()
 
     def attend_pair(j, carry):
-        @pl.when(j + 4 < CHUNKS)
-        def _():
-            own_chunk(j + 4)
-            mate_chunk(j + 2)
+        @pl.when(j + 6 < CHUNKS)
+        def _():
+            own_chunk(j + 6)
+
+        mate_chunk(j + 3)
 
         pl.when(j == 1)(send_share)
         pl.when(j > 1)(lambda: other_half(j - 2))
         attend([(2 * j + i, edge) for i in range(2) for edge in edges])
-        pl.when(is_outer)(lambda: att_copy(j).start())
         return carry
 
     lax.fori_loop(0, pairs, attend_pair, 0)
-    mate_chunk(CHUNKS - 2)
-    mate_chunk(CHUNKS - 1)
-    other_half(pairs - 2)
-    other_half(pairs - 1)
+
+    @pl.when(is_outer)
+    def _():
+        att_copy(1).start()
+        att_copy(2).start()
+
+    other_half(2)
 
     for step in range(1, group):
         owner = lax.rem(me + step, group)
@@ -379,13 +399,13 @@
         out_copy(k).start()
 
     def project(k, carry):
-        pl.when((k + 1 >= pairs) & (k + 1 < CHUNKS))(lambda: other_half(k + 1))
+        pl.when((k + 1 >= 3) & (k + 1 < CHUNKS))(lambda: other_half(k + 1))
         from_side(k)
 
         @pl.when(k == OUTER)
         def _():
-            for j in range(pairs):
-                att_copy(j).wait_recv()
+            for i in range(3):
+                att_copy(i).wait_recv()
 
         @pl.when(k >= OUTER)
         def _():
@@ -396,6 +416,7 @@
             out_copy(k).start()
 
         pl.when(k < OUTER)(lambda: own_rows(k))
+        pl.when(k == 4)(lambda: mate_chunk(CHUNKS - 1))
         return carry
 
     @pl.when(is_inner)
@@ -440,8 +461,8 @@
 
     @pl.when(is_outer)
     def _():
-        for j in range(pairs):
-            att_copy(j).wait_send()
+        for i in range(3):
+            att_copy(i).wait_send()
 
     pl.when(has_up)(lambda: halo(0).wait_send())
     pl.when(has_down)(lambda: halo(1).wait_send())
@@ -501,8 +522,8 @@
             dma((n_row, CHUNKS)),
             dma((n_col - 1, n_row, CHUNKS)),
             dma((group, CHUNKS)),
-            dma((inner // HDIM // 2,)),
-            dma((inner // HDIM // 2,)),
+            dma((3,)),
+            dma((3,)),
             dma((CHUNKS,)),
             dma((CHUNKS,)),
             dma((2,)),

time: 54.2 us -> 52.2 us (0.963)
  Pallas kernels: 52.4 us -> 50.5 us
    pallas_call x1, Pallas kernels: 52.4 us -> 50.5 us  [layer(): pl.pallas_call(functools.partial(kernel, sizes, distance), out_shape=jax....]
where the time goes in v6:
time: 52.2 us; the launch traced here: 52.1 us
  Pallas kernels  50.5 us (97%)
  local copies, waits for them, and re-layouts  0.88 us (2%)
  between operations  0.68 us (1%)
    pallas_call x1, Pallas kernels, layer(): pl.pallas_call(functools.partial(kernel, sizes, distance), out_shape=jax....  50.5 us

profile of v6, /device:TPU:0, one launch (start us, length us, event | category | flops | bytes accessed | tf_op | source)
XLA Modules:
  0.0 52.1 jit_solution(16847056062363353661)
XLA Ops:
  0.7 50.5 %conditional.1 = (bf16[1,12,16,2048]{3,2,1,0:T(8,128)(2,1)S(1)}) conditional(s32[]{:T(128)} %clamp.3, (bf16[1,12,16,1024]{3,2,1,0:T(8,128)(2,1)}, bf16[1,2,12,16,1024]{4,3,2,1,0:T(8,128)(2,1)}, bf16[1,128,2048]{2,1,0:T(8,128)(2,1)}, bf16[1,256,2048]{2,1,0:T(8,128)(2,1)}, bf16[1,1000,256]{2,1,0:T(8,128)(2,1)}, /*index=5*/s32[1]{0:T(128)}, ...), branch_computations={%region_0.1_spmd, %region_1.2_spmd} | conditional | flops 805306368 | bytes 4194312 | solution.py:553
  0.7 50.5 %sublayer_distance_1.1 = bf16[192,2048]{1,0:T(8,128)(2,1)S(1)} custom-call(bf16[1,12,16,1024]{3,2,1,0:T(8,128)(2,1)} %get-tuple-element.37.q_hbm, bf16[1,2,12,16,1024]{4,3,2,1,0:T(8,128)(2,1)} %get-tuple-element.38.kv_hbm, bf16[1,128,2048]{2,1,0:T(8,128)(2,1)} %get-tuple-element.39.o_hbm, bf16[1,256,2048]{2,1,0:T(8,128)(2,1)} %get-tuple-element.40.g_hbm, ...), custom_call_target="tpu_custom_call" | custom-call | flops 805306368 | bytes 4194304 | tf_op jit(solution)/shard_map/cond/branch_0_fun/sublayer_distance_1/pallas_call | solution.py:493
  51.2 0.9 %copy.15 = bf16[1,12,16,2048]{3,2,1,0:T(8,128)(2,1)} copy(bf16[1,12,16,2048]{3,2,1,0:T(8,128)(2,1)S(1)} %get-tuple-element.51) | data formatting | bytes 1572864

commit v7 on v6

--- a/solution.py
+++ b/solution.py
@@ -12,7 +12,7 @@
 RADIUS = 3
 CHUNKS = 8
 AHEAD = 3
-OUTER = 3
+OUTER = 5
 MESH = pl.DeviceIdType.MESH
 F32 = jnp.float32
 BF16 = jnp.bfloat16
@@ -351,7 +351,7 @@
         mate_chunk(j + 3)
 
         pl.when(j == 1)(send_share)
-        pl.when(j > 1)(lambda: other_half(j - 2))
+        other_half(j)
         attend([(2 * j + i, edge) for i in range(2) for edge in edges])
         return carry
 
@@ -362,7 +362,7 @@
         att_copy(1).start()
         att_copy(2).start()
 
-    other_half(2)
+    mate_chunk(CHUNKS - 1)
 
     for step in range(1, group):
         owner = lax.rem(me + step, group)
@@ -399,7 +399,7 @@
         out_copy(k).start()
 
     def project(k, carry):
-        pl.when((k + 1 >= 3) & (k + 1 < CHUNKS))(lambda: other_half(k + 1))
+        pl.when((k + 1 >= pairs) & (k + 1 < CHUNKS))(lambda: other_half(k + 1))
         from_side(k)
 
         @pl.when(k == OUTER)
@@ -416,7 +416,6 @@
             out_copy(k).start()
 
         pl.when(k < OUTER)(lambda: own_rows(k))
-        pl.when(k == 4)(lambda: mate_chunk(CHUNKS - 1))
         return carry
 
     @pl.when(is_inner)
@@ -425,13 +424,14 @@
 
     @pl.when(is_outer)
     def _():
-        for k in range(OUTER):
-            for row in (mate, n_row - 1 - mate, n_row - 1 - r):
-                back_copy(row, k).wait_recv()
-                spread(row, k)
-        for k in range(OUTER):
-            from_side(k)
-            own_rows(k)
+        for k in range(OUTER + 1):
+            if k < OUTER:
+                for row in (mate, n_row - 1 - mate, n_row - 1 - r):
+                    back_copy(row, k).wait_recv()
+                    spread(row, k)
+            if k > 0:
+                from_side(k - 1)
+                own_rows(k - 1)
         for k in range(OUTER, CHUNKS):
             mate_copy(k).wait_recv()
 

time: 52.2 us -> 49.7 us (0.952)
  Pallas kernels: 50.5 us -> 48 us
    pallas_call x1, Pallas kernels: 50.5 us -> 48 us  [layer(): pl.pallas_call(functools.partial(kernel, sizes, distance), out_shape=jax....]
where the time goes in v7:
time: 49.7 us; the launch traced here: 49.6 us
  Pallas kernels  48 us (97%)
  local copies, waits for them, and re-layouts  0.88 us (2%)
  between operations  0.68 us (1%)
    pallas_call x1, Pallas kernels, layer(): pl.pallas_call(functools.partial(kernel, sizes, distance), out_shape=jax....  48 us

profile of v7, /device:TPU:0, one launch (start us, length us, event | category | flops | bytes accessed | tf_op | source)
XLA Modules:
  0.0 49.6 jit_solution(8875747399911900303)
XLA Ops:
  0.7 48.0 %conditional.1 = (bf16[1,12,16,2048]{3,2,1,0:T(8,128)(2,1)S(1)}) conditional(s32[]{:T(128)} %clamp.3, (bf16[1,12,16,1024]{3,2,1,0:T(8,128)(2,1)}, bf16[1,2,12,16,1024]{4,3,2,1,0:T(8,128)(2,1)}, bf16[1,128,2048]{2,1,0:T(8,128)(2,1)}, bf16[1,256,2048]{2,1,0:T(8,128)(2,1)}, bf16[1,1000,256]{2,1,0:T(8,128)(2,1)}, /*index=5*/s32[1]{0:T(128)}, ...), branch_computations={%region_0.1_spmd, %region_1.2_spmd} | conditional | flops 805306368 | bytes 4194312 | solution.py:553
  0.7 48.0 %sublayer_distance_1.1 = bf16[192,2048]{1,0:T(8,128)(2,1)S(1)} custom-call(bf16[1,12,16,1024]{3,2,1,0:T(8,128)(2,1)} %get-tuple-element.37.q_hbm, bf16[1,2,12,16,1024]{4,3,2,1,0:T(8,128)(2,1)} %get-tuple-element.38.kv_hbm, bf16[1,128,2048]{2,1,0:T(8,128)(2,1)} %get-tuple-element.39.o_hbm, bf16[1,256,2048]{2,1,0:T(8,128)(2,1)} %get-tuple-element.40.g_hbm, ...), custom_call_target="tpu_custom_call" | custom-call | flops 805306368 | bytes 4194304 | tf_op jit(solution)/shard_map/cond/branch_0_fun/sublayer_distance_1/pallas_call | solution.py:493
  48.7 0.9 %copy.15 = bf16[1,12,16,2048]{3,2,1,0:T(8,128)(2,1)} copy(bf16[1,12,16,2048]{3,2,1,0:T(8,128)(2,1)S(1)} %get-tuple-element.51) | data formatting | bytes 1572864

commit v8 on v7

--- a/solution.py
+++ b/solution.py
@@ -30,7 +30,7 @@
     out_hbm,
     q_buf, kv_buf, bias_mid, bias_edge, att, o_own, o_peer, w_buf, out_buf, g_buf, t_buf,
     pack_out, pack_in, reply_out, reply_in, gates, gate_sum, mate_out,
-    local_sem, out_sem, gossip_send, gossip_recv, w_send, w_back, w_side, w_recv, att_send, att_recv, mate_send, mate_recv,
+    local_sem, out_sem, gossip_send, gossip_recv, w_send, w_back, w_side, w_side_recv, w_recv, att_send, att_recv, mate_send, mate_recv,
     halo_send, halo_recv, side_send, side_recv, note_send, note_recv, gate_send, gate_recv,
 ):
     n_dp, n_row, n_col = sizes
@@ -53,6 +53,8 @@
     is_inner = jnp.logical_not(is_outer)
     mate = r + 1 - 2 * lax.rem(r, 2)
     onward = 1 + lax.rem(r, 2)
+    near = r - lax.rem(r, 2)
+    far = n_row - 2 - near
     tokens = tile_rows * tile_cols
 
     def col_of(step):
@@ -172,23 +174,33 @@
     for q_start, q_rows, k_start, mask in (middle,) + edges:
         mask[...] = allowed(q_start, q_rows, k_start)
 
-    def w_copy(owner, k, sem, **where):
-        rows = pl.ds(pl.multiple_of(owner * shard, shard), shard)
-        place = w_buf.at[k, rows]
-        return remote(place, place, sem, w_recv.at[owner, k], **where)
+    def place(k, row, count, col):
+        return w_buf.at[k, pl.ds(row, count), col]
 
     def onward_copy(row, k):
-        return w_copy(row * n_col + c, k, w_send.at[row, k], row=onward)
-
-    def back_copy(row, k):
-        return w_copy(row * n_col + c, k, w_back.at[row, k], row=mate)
-
-    def side_copy(row, k, step):
-        return w_copy(row * n_col + c, k, w_side.at[step - 1, row, k], col=col_of(step))
-
-    def spread(row, k):
+        here = place(k, row, 1, c)
+        return remote(here, here, w_send.at[row, k], w_recv.at[row, k], row=onward)
+
+    def back_copy(which, row, count, k):
+        here = place(k, row, count, c)
+        return remote(here, here, w_back.at[which, k], w_recv.at[row, k], row=mate)
+
+    def side_copy(which, row, count, k, step):
+        here = place(k, row, count, c)
+        return remote(
+            here, here, w_side.at[step - 1, which, k], w_side_recv.at[step - 1, which, k], col=col_of(step)
+        )
+
+    def spread(which, row, count, k):
         for step in range(1, n_col):
-            side_copy(row, k, step).start()
+            side_copy(which, row, count, k, step).start()
+
+    def from_side(which, row, count, k):
+        for step in range(1, n_col):
+            there = place(k, row, count, col_of(n_col - step))
+            remote(
+                there, there, w_side.at[step - 1, which, k], w_side_recv.at[step - 1, which, k], col=col_of(step)
+            ).wait_recv()
 
     def own_chunk(k):
         gossip(k).wait_recv()
@@ -200,21 +212,16 @@
 
         columns = pl.ds(pl.multiple_of(k * cut, cut), cut)
         both = o_own[:, columns].astype(F32) + o_peer[k].astype(F32)
-        w_buf[k, pl.ds(pl.multiple_of(me * shard, shard), shard), :] = (0.5 * both).astype(BF16)
+        w_buf[k, r, c] = (0.5 * both).astype(BF16)
         onward_copy(r, k).start()
-        pl.when(is_inner | (k < OUTER))(lambda: spread(r, k))
-        pl.when(is_inner & (k < OUTER))(lambda: back_copy(r, k).start())
-
-    def hand_on(row, k):
-        onward_copy(row, k).wait_recv()
-        spread(row, k)
+        pl.when(is_inner & (k < OUTER))(lambda: back_copy(0, r, 1, k).start())
 
     def mate_chunk(k):
         @pl.when(is_inner)
         def _():
             onward_copy(mate, k).wait_recv()
             onward_copy(mate, k).start()
-            spread(mate, k)
+            spread(0, near, 2, k)
 
     scale = 1.0 / math.sqrt(HDIM)
 
@@ -234,12 +241,16 @@
             scores.append(score + mask[...])
         tops = [jnp.max(score, axis=1, keepdims=True) for score in scores]
         weights = [jnp.exp((score - top) * scale) for score, top in zip(scores, tops)]
-        totals = [jnp.sum(weight, axis=1, keepdims=True) for weight in weights]
+        ones = jnp.ones((tile_rows * wide, HDIM), BF16)
         sums = [
-            jnp.dot(weight.astype(BF16), near_rows(1, head, k_start), preferred_element_type=F32)
+            jnp.dot(
+                weight.astype(BF16),
+                jnp.concatenate([near_rows(1, head, k_start), ones], axis=1),
+                preferred_element_type=F32,
+            )
             for weight, (head, (_, _, k_start, _)) in zip(weights, parts)
         ]
-        means = [(part / total).astype(BF16) for part, total in zip(sums, totals)]
+        means = [(both[:, :HDIM] / both[:, HDIM:]).astype(BF16) for both in sums]
         for mean, (head, (q_start, q_rows, _, _)) in zip(means, parts):
             att[pl.ds(q_start * tile_cols, q_rows * tile_cols), lanes(head)] = mean
 
@@ -325,9 +336,10 @@
     def other_half(k):
         @pl.when(is_inner)
         def _():
-            for row in (n_row - 1 - r, n_row - 1 - mate):
-                hand_on(row, k)
-                pl.when(k < OUTER)(lambda row=row: back_copy(row, k).start())
+            onward_copy(n_row - 1 - r, k).wait_recv()
+            onward_copy(n_row - 1 - mate, k).wait_recv()
+            spread(1, far, 2, k)
+            pl.when(k < OUTER)(lambda: back_copy(1, far, 2, k).start())
 
     def gate_copy(owner, step):
         other = lax.rem(me + step, group)
@@ -384,14 +396,8 @@
             mate_send.at[k], mate_recv.at[k], row=mate,
         )
 
-    def from_side(k):
-        for row in range(n_row):
-            for step in range(1, n_col):
-                owner = row * n_col + col_of(step)
-                w_copy(owner, k, w_side.at[step - 1, row, k], col=col_of(step)).wait_recv()
-
     def rows_of(count, k):
-        product = jnp.dot(att[pl.ds(0, count)], w_buf[k], preferred_element_type=F32)
+        product = jnp.dot(att[pl.ds(0, count)], w_buf[k].reshape(inner, cut), preferred_element_type=F32)
         return (gate_sum[k] * product).astype(BF16)
 
     def own_rows(k):
@@ -400,7 +406,8 @@
 
     def project(k, carry):
         pl.when((k + 1 >= pairs) & (k + 1 < CHUNKS))(lambda: other_half(k + 1))
-        from_side(k)
+        from_side(0, near, 2, k)
+        from_side(1, far, 2, k)
 
         @pl.when(k == OUTER)
         def _():
@@ -426,11 +433,11 @@
     def _():
         for k in range(OUTER + 1):
             if k < OUTER:
-                for row in (mate, n_row - 1 - mate, n_row - 1 - r):
-                    back_copy(row, k).wait_recv()
-                    spread(row, k)
+                back_copy(0, mate, 1, k).wait_recv()
+                back_copy(1, far, 2, k).wait_recv()
+                spread(0, 0, n_row, k)
             if k > 0:
-                from_side(k - 1)
+                from_side(0, 0, n_row, k - 1)
                 own_rows(k - 1)
         for k in range(OUTER, CHUNKS):
             mate_copy(k).wait_recv()
@@ -438,22 +445,25 @@
     def sent(k, carry):
         onward_copy(r, k).wait_send()
 
-        @pl.when(is_inner | (k < OUTER))
-        def _():
-            out_copy(k).wait()
-            for row in range(n_row):
-                for step in range(1, n_col):
-                    side_copy(row, k, step).wait_send()
+        pl.when(is_inner | (k < OUTER))(lambda: out_copy(k).wait())
+
+        @pl.when(is_outer & (k < OUTER))
+        def _():
+            for step in range(1, n_col):
+                side_copy(0, 0, n_row, k, step).wait_send()
 
         @pl.when(is_inner)
         def _():
             onward_copy(mate, k).wait_send()
+            for step in range(1, n_col):
+                side_copy(0, near, 2, k, step).wait_send()
+                side_copy(1, far, 2, k, step).wait_send()
             pl.when(k >= OUTER)(lambda: mate_copy(k).wait_send())
 
             @pl.when(k < OUTER)
             def _():
-                for row in (r, n_row - 1 - r, n_row - 1 - mate):
-                    back_copy(row, k).wait_send()
+                back_copy(0, r, 1, k).wait_send()
+                back_copy(1, far, 2, k).wait_send()
 
         return carry
 
@@ -503,7 +513,7 @@
             pltpu.VMEM((2 * tokens, inner), BF16),
             pltpu.VMEM((shard, width), BF16),
             pltpu.VMEM((CHUNKS, shard, cut), BF16),
-            pltpu.VMEM((CHUNKS, group * shard, cut), BF16),
+            pltpu.VMEM((CHUNKS, n_row, n_col, shard, cut), BF16),
             pltpu.VMEM((CHUNKS, tokens, cut), BF16),
             pltpu.VMEM((span, width), BF16),
             pltpu.VMEM((classes, span), BF16),
@@ -519,9 +529,10 @@
             dma((CHUNKS,)),
             dma((CHUNKS,)),
             dma((n_row, CHUNKS)),
+            dma((2, CHUNKS)),
+            dma((n_col - 1, 2, CHUNKS)),
+            dma((n_col - 1, 2, CHUNKS)),
             dma((n_row, CHUNKS)),
-            dma((n_col - 1, n_row, CHUNKS)),
-            dma((group, CHUNKS)),
             dma((3,)),
             dma((3,)),
             dma((CHUNKS,)),

time: 49.7 us -> 48.6 us (0.978)
  Pallas kernels: 48 us -> 47.4 us
    pallas_call x1, Pallas kernels: 48 us -> 47.4 us  [layer(): pl.pallas_call(functools.partial(kernel, sizes, distance), out_shape=jax....]
where the time goes in v8:
time: 48.6 us; the launch traced here: 48.9 us
  Pallas kernels  47.4 us (98%)
  local copies, waits for them, and re-layouts  0.88 us (2%)
  between operations  0.68 us (1%)
    pallas_call x1, Pallas kernels, layer(): pl.pallas_call(functools.partial(kernel, sizes, distance), out_shape=jax....  47.4 us

profile of v8, /device:TPU:0, one launch (start us, length us, event | category | flops | bytes accessed | tf_op | source)
XLA Modules:
  0.0 48.9 jit_solution(6060497539571984629)
XLA Ops:
  0.7 47.4 %conditional.1 = (bf16[1,12,16,2048]{3,2,1,0:T(8,128)(2,1)S(1)}) conditional(s32[]{:T(128)} %clamp.3, (bf16[1,12,16,1024]{3,2,1,0:T(8,128)(2,1)}, bf16[1,2,12,16,1024]{4,3,2,1,0:T(8,128)(2,1)}, bf16[1,128,2048]{2,1,0:T(8,128)(2,1)}, bf16[1,256,2048]{2,1,0:T(8,128)(2,1)}, bf16[1,1000,256]{2,1,0:T(8,128)(2,1)}, /*index=5*/s32[1]{0:T(128)}, ...), branch_computations={%region_0.1_spmd, %region_1.2_spmd} | conditional | flops 805306368 | bytes 4194312 | solution.py:564
  0.7 47.4 %sublayer_distance_1.1 = bf16[192,2048]{1,0:T(8,128)(2,1)S(1)} custom-call(bf16[1,12,16,1024]{3,2,1,0:T(8,128)(2,1)} %get-tuple-element.37.q_hbm, bf16[1,2,12,16,1024]{4,3,2,1,0:T(8,128)(2,1)} %get-tuple-element.38.kv_hbm, bf16[1,128,2048]{2,1,0:T(8,128)(2,1)} %get-tuple-element.39.o_hbm, bf16[1,256,2048]{2,1,0:T(8,128)(2,1)} %get-tuple-element.40.g_hbm, ...), custom_call_target="tpu_custom_call" | custom-call | flops 805306368 | bytes 4194304 | tf_op jit(solution)/shard_map/cond/branch_0_fun/sublayer_distance_1/pallas_call | solution.py:503
  48.0 0.9 %copy.15 = bf16[1,12,16,2048]{3,2,1,0:T(8,128)(2,1)} copy(bf16[1,12,16,2048]{3,2,1,0:T(8,128)(2,1)S(1)} %get-tuple-element.51) | data formatting | bytes 1572864

commit v9 on v8

--- a/solution.py
+++ b/solution.py
@@ -276,32 +276,28 @@
 
     quarter = heads // 4
 
-    def attend_middle(i):
-        attend([(head, middle) for head in range(i * quarter, (i + 1) * quarter)])
-
-    own_chunk(1)
-    attend_middle(0)
-    own_chunk(2)
-    attend_middle(1)
-
-    @pl.when(has_down)
-    def _():
-        halo(0).wait_recv()
-        for i in range(len(sides)):
-            corner(0, i).start()
-
-    @pl.when(has_up)
-    def _():
-        halo(1).wait_recv()
-        for i in range(len(sides)):
-            corner(1, i).start()
-
-    own_chunk(3)
-    mate_chunk(0)
-    attend_middle(2)
-    own_chunk(4)
-    mate_chunk(1)
-    attend_middle(3)
+    def middle_step(i, carry):
+        own_chunk(i + 1)
+
+        @pl.when(i == 2)
+        def _():
+            @pl.when(has_down)
+            def _():
+                halo(0).wait_recv()
+                for i in range(len(sides)):
+                    corner(0, i).start()
+
+            @pl.when(has_up)
+            def _():
+                halo(1).wait_recv()
+                for i in range(len(sides)):
+                    corner(1, i).start()
+
+        pl.when(i > 1)(lambda: mate_chunk(i - 2))
+        attend([(i * quarter + n, middle) for n in range(quarter)])
+        return carry
+
+    lax.fori_loop(0, 4, middle_step, 0)
     pl.when(is_outer)(lambda: att_copy(0).start())
     own_chunk(5)
     mate_chunk(2)
@@ -431,14 +427,21 @@
 
     @pl.when(is_outer)
     def _():
-        for k in range(OUTER + 1):
-            if k < OUTER:
+        def outer_step(k, carry):
+            @pl.when(k < OUTER)
+            def _():
                 back_copy(0, mate, 1, k).wait_recv()
                 back_copy(1, far, 2, k).wait_recv()
                 spread(0, 0, n_row, k)
-            if k > 0:
+
+            @pl.when(k > 0)
+            def _():
                 from_side(0, 0, n_row, k - 1)
                 own_rows(k - 1)
+
+            return carry
+
+        lax.fori_loop(0, OUTER + 1, outer_step, 0)
         for k in range(OUTER, CHUNKS):
             mate_copy(k).wait_recv()
 

time: 48.6 us -> 49.1 us (1.010); the launches traced: 48.9 us -> 48.9 us
  no operation moved by 1% of the time
where the time goes in v9:
time: 49.1 us; the launch traced here: 48.9 us
  Pallas kernels  47.3 us (96%)
  local copies, waits for them, and re-layouts  0.88 us (2%)
  between operations  0.68 us (1%)
    pallas_call x1, Pallas kernels, layer(): pl.pallas_call(functools.partial(kernel, sizes, distance), out_shape=jax....  47.3 us

profile of v9, /device:TPU:0, one launch (start us, length us, event | category | flops | bytes accessed | tf_op | source)
XLA Modules:
  0.0 48.9 jit_solution(6671339202251879123)
XLA Ops:
  0.7 47.3 %conditional.1 = (bf16[1,12,16,2048]{3,2,1,0:T(8,128)(2,1)S(1)}) conditional(s32[]{:T(128)} %clamp.3, (bf16[1,12,16,1024]{3,2,1,0:T(8,128)(2,1)}, bf16[1,2,12,16,1024]{4,3,2,1,0:T(8,128)(2,1)}, bf16[1,128,2048]{2,1,0:T(8,128)(2,1)}, bf16[1,256,2048]{2,1,0:T(8,128)(2,1)}, bf16[1,1000,256]{2,1,0:T(8,128)(2,1)}, /*index=5*/s32[1]{0:T(128)}, ...), branch_computations={%region_0.1_spmd, %region_1.2_spmd} | conditional | flops 805306368 | bytes 4194312 | solution.py:567
  0.7 47.3 %sublayer_distance_1.1 = bf16[192,2048]{1,0:T(8,128)(2,1)S(1)} custom-call(bf16[1,12,16,1024]{3,2,1,0:T(8,128)(2,1)} %get-tuple-element.37.q_hbm, bf16[1,2,12,16,1024]{4,3,2,1,0:T(8,128)(2,1)} %get-tuple-element.38.kv_hbm, bf16[1,128,2048]{2,1,0:T(8,128)(2,1)} %get-tuple-element.39.o_hbm, bf16[1,256,2048]{2,1,0:T(8,128)(2,1)} %get-tuple-element.40.g_hbm, ...), custom_call_target="tpu_custom_call" | custom-call | flops 805306368 | bytes 4194304 | tf_op jit(solution)/shard_map/cond/branch_0_fun/sublayer_distance_1/pallas_call | solution.py:506
  48.0 0.9 %copy.15 = bf16[1,12,16,2048]{3,2,1,0:T(8,128)(2,1)} copy(bf16[1,12,16,2048]{3,2,1,0:T(8,128)(2,1)S(1)} %get-tuple-element.51) | data formatting | bytes 1572864

commit v10 on v9

--- a/solution.py
+++ b/solution.py
@@ -298,7 +298,6 @@
         return carry
 
     lax.fori_loop(0, 4, middle_step, 0)
-    pl.when(is_outer)(lambda: att_copy(0).start())
     own_chunk(5)
     mate_chunk(2)
 
@@ -358,6 +357,7 @@
 
         mate_chunk(j + 3)
 
+        pl.when((j == 1) & is_outer)(lambda: att_copy(0).start())
         pl.when(j == 1)(send_share)
         other_half(j)
         attend([(2 * j + i, edge) for i in range(2) for edge in edges])

time: 49.1 us -> 49.1 us (level)
  no operation moved by 1% of the time
where the time goes in v10:
time: 49.1 us; the launch traced here: 48.9 us
  Pallas kernels  47.3 us (96%)
  local copies, waits for them, and re-layouts  0.88 us (2%)
  between operations  0.68 us (1%)
    pallas_call x1, Pallas kernels, layer(): pl.pallas_call(functools.partial(kernel, sizes, distance), out_shape=jax....  47.3 us

profile of v10, /device:TPU:0, one launch (start us, length us, event | category | flops | bytes accessed | tf_op | source)
XLA Modules:
  0.0 48.9 jit_solution(7460330274607404129)
XLA Ops:
  0.7 47.3 %conditional.1 = (bf16[1,12,16,2048]{3,2,1,0:T(8,128)(2,1)S(1)}) conditional(s32[]{:T(128)} %clamp.3, (bf16[1,12,16,1024]{3,2,1,0:T(8,128)(2,1)}, bf16[1,2,12,16,1024]{4,3,2,1,0:T(8,128)(2,1)}, bf16[1,128,2048]{2,1,0:T(8,128)(2,1)}, bf16[1,256,2048]{2,1,0:T(8,128)(2,1)}, bf16[1,1000,256]{2,1,0:T(8,128)(2,1)}, /*index=5*/s32[1]{0:T(128)}, ...), branch_computations={%region_0.1_spmd, %region_1.2_spmd} | conditional | flops 805306368 | bytes 4194312 | solution.py:567
  0.7 47.3 %sublayer_distance_1.1 = bf16[192,2048]{1,0:T(8,128)(2,1)S(1)} custom-call(bf16[1,12,16,1024]{3,2,1,0:T(8,128)(2,1)} %get-tuple-element.37.q_hbm, bf16[1,2,12,16,1024]{4,3,2,1,0:T(8,128)(2,1)} %get-tuple-element.38.kv_hbm, bf16[1,128,2048]{2,1,0:T(8,128)(2,1)} %get-tuple-element.39.o_hbm, bf16[1,256,2048]{2,1,0:T(8,128)(2,1)} %get-tuple-element.40.g_hbm, ...), custom_call_target="tpu_custom_call" | custom-call | flops 805306368 | bytes 4194304 | tf_op jit(solution)/shard_map/cond/branch_0_fun/sublayer_distance_1/pallas_call | solution.py:506
  48.0 0.9 %copy.15 = bf16[1,12,16,2048]{3,2,1,0:T(8,128)(2,1)} copy(bf16[1,12,16,2048]{3,2,1,0:T(8,128)(2,1)S(1)} %get-tuple-element.51) | data formatting | bytes 1572864
